TPU v7x, 32 devices: a whole 2x2x4 slice. The times are simulated.
32 devices in a mesh: row: 8 (over y, x, core), col: 4 (over z).
Axes of the slice: x: 2, y: 2, z: 4, core: 2. Of those that a mesh axis runs over, the one named last changes fastest.
Arguments:
- block_tiles: bfloat16 [8, 4, 32, 128, 128], P('row', 'col'), may hold values from -1.1953125 to 1.1953125
- block_index: int32 [8, 4, 32, 2], P('row', 'col'), may hold values from -1 to 127, as said below
Outputs:
- product: bfloat16 [8, 4, 32, 128, 128], P('row', 'col')
Inputs may be any that keep to these rules, and one draw needn't show every extreme that they name: `block_index`: block numbers run within one matrix. Positions of rows v > c hold only empty slots; v = c holds the 32 diagonal blocks of its region; v < c holds 32 blocks of its region, exactly one in each block row and in each block column of the region. Slots are all live or all empty at a position, in any order. In the symmetric matrix every block row has exactly one nonzero block in each region of 32 block columns, and the pattern is closed: if X(i,k) and X(i,j) are nonzero then so is X(k,j), so the blocks form 32 chains that each hold one block row of every region.
All inputs are finite; a program needn't handle non-finite values.
Results may differ from a plain program's by a relative error of at most 0.0023.
Values may be sent and summed in bfloat16 or wider, within the bound.
No kernel may reach another device: no remote copies, remote signals or barrier semaphores. Data moves between devices by JAX's collectives and lax.ppermute only.
A program may use at most 64 MiB of HBM per device.

v0:
```python
import jax
import jax.numpy as jnp
from jax import lax
from jax.sharding import PartitionSpec as P

STEPS = 4


def from_behind(value, axis, by):
    size = lax.axis_size(axis)
    return lax.ppermute(value, axis, [(i, (i + by) % size) for i in range(size)])


def for_sending(value):

    def short(part):
        return part.astype(jnp.bfloat16) if part.dtype == jnp.float32 else part

    return jax.tree.map(short, value)


def assemble(own_tiles, own_index, mirror_tiles, mirror_index):
    own_valid = own_index[:, 0] >= 0
    on_diagonal = own_index[:, 0] == own_index[:, 1]
    widened = own_tiles.astype(jnp.float32)
    symmetric = ((widened + jnp.swapaxes(widened, 1, 2)) * 0.5).astype(jnp.bfloat16)
    own_kept = jnp.where(on_diagonal[:, None, None], symmetric, own_tiles)
    mirror_valid = (mirror_index[:, 0] >= 0) & (mirror_index[:, 0] != mirror_index[:, 1])
    flipped = jnp.swapaxes(mirror_tiles, 1, 2)
    zero_tiles = jnp.zeros_like(own_tiles)
    merged = jnp.where(
        own_valid[:, None, None],
        own_kept,
        jnp.where(mirror_valid[:, None, None], flipped, zero_tiles),
    )
    swapped_index = mirror_index[:, ::-1]
    empty_index = jnp.full_like(own_index, -1)
    merged_index = jnp.where(
        own_valid[:, None], own_index, jnp.where(mirror_valid[:, None], swapped_index, empty_index)
    )
    return (merged, merged_index)


def multiply(left_tiles, left_index, right_tiles, right_index, out_index, totals):
    target_row = out_index[:, 0]
    target_col = out_index[:, 1]
    left_match = (left_index[None, :, 0] == target_row[:, None]) & (target_row[:, None] >= 0)
    left_found = jnp.any(left_match, axis=1)
    left_slot = jnp.argmax(left_match.astype(jnp.int32), axis=1)
    inner_block = jnp.take(left_index[:, 1], left_slot)
    right_match = (right_index[None, :, 0] == inner_block[:, None]) & (
        right_index[None, :, 1] == target_col[:, None]
    )
    right_found = jnp.any(right_match, axis=1)
    right_slot = jnp.argmax(right_match.astype(jnp.int32), axis=1)
    usable = left_found & right_found
    chosen_left = jnp.where(
        usable[:, None, None],
        jnp.take(left_tiles, left_slot, axis=0),
        jnp.zeros((), left_tiles.dtype),
    )
    chosen_right = jnp.take(right_tiles, right_slot, axis=0)
    return totals + jnp.einsum(
        "uxy,uyz->uxz", chosen_left, chosen_right, preferred_element_type=jnp.float32
    )


def rotate_columns(panel, amount, bit_count):
    for bit_level in range(bit_count):
        arrived = from_behind((panel[0], panel[1]), "col", -(1 << bit_level))
        chosen = amount >> bit_level & 1 == 1
        panel = (jnp.where(chosen, arrived[0], panel[0]), jnp.where(chosen, arrived[1], panel[1]))
    return panel


def rotate_rows(panel, amount, bit_count, stride):
    for bit_level in range(bit_count):
        arrived = from_behind((panel[0], panel[1]), "row", -(1 << bit_level) * stride)
        chosen = amount >> bit_level & 1 == 1
        panel = (jnp.where(chosen, arrived[0], panel[0]), jnp.where(chosen, arrived[1], panel[1]))
    return panel


def on_device(block_tiles, block_index):
    row_count = lax.axis_size("row")
    groups = lax.axis_size("col")
    systems = row_count // groups
    own_tiles = block_tiles[0, 0]
    own_index = block_index[0, 0]
    slot_count = own_tiles.shape[0]
    tile_width = own_tiles.shape[1]
    virtual_row = lax.axis_index("row") // systems
    column = lax.axis_index("col")
    piece_rows = slot_count // row_count
    scattered = (
        lax.all_to_all(
            lax.all_to_all(
                own_tiles.reshape(row_count, piece_rows, tile_width, tile_width),
                "row",
                split_axis=0,
                concat_axis=0,
                tiled=True,
            ),
            "col",
            split_axis=0,
            concat_axis=0,
            tiled=True,
        ),
        lax.all_to_all(
            lax.all_to_all(
                own_index.reshape(row_count, piece_rows, 2),
                "row",
                split_axis=0,
                concat_axis=0,
                tiled=True,
            ),
            "col",
            split_axis=0,
            concat_axis=0,
            tiled=True,
        ),
    )
    landed = (
        lax.all_to_all(scattered[0], "row", split_axis=0, concat_axis=0, tiled=True),
        lax.all_to_all(scattered[1], "row", split_axis=0, concat_axis=0, tiled=True),
    )
    region = assemble(
        own_tiles,
        own_index,
        landed[0].reshape(slot_count, tile_width, tile_width),
        landed[1].reshape(slot_count, 2),
    )
    bit_count = (groups - 1).bit_length()
    left_panel = rotate_columns(region, virtual_row, bit_count)
    right_panel = rotate_rows(region, column, bit_count, systems)
    accumulated = jnp.zeros((slot_count, tile_width, tile_width), jnp.float32)
    for step_index in range(STEPS):
        if step_index + 1 < STEPS:
            next_left = from_behind((left_panel[0], for_sending(left_panel[1])), "col", -1)
            next_right = from_behind((right_panel[0], for_sending(right_panel[1])), "row", -systems)
        accumulated = multiply(
            left_panel[0], left_panel[1], right_panel[0], right_panel[1], own_index, accumulated
        )
        if step_index + 1 < STEPS:
            left_panel = next_left
            right_panel = next_right
    own_valid = own_index[:, 0] >= 0
    result = jnp.where(own_valid[:, None, None], accumulated, jnp.zeros((), jnp.float32)).astype(
        jnp.bfloat16
    )
    return result[None, None]


def solution(mesh):
    in_specs = (P("row", "col", None, None, None), P("row", "col", None, None))
    out_specs = P("row", "col", None, None, None)
    return jax.shard_map(
        on_device, mesh=mesh, in_specs=in_specs, out_specs=out_specs, check_vma=False
    )
```

profile of v0, /device:TPU:0, one launch (start us, length us, event | category | flops | bytes accessed | tf_op | source)
XLA Modules:
  0.0 270.9 jit_solution(18221617782562952159)
XLA Ops:
  0.0 0.8 reshape_squeeze.6
  1.4 5.2 %all-to-all-start = ((s32[8,4,2]{1,2,0:T(2,128)}), s32[8,4,2]{1,2,0:T(2,128)}, u32[]{:S(2)}, u32[]{:S(2)}) async-start(s32[8,4,2]{1,2,0:T(2,128)} %copy.11), calls=%async_computation | async-start | bytes 16384 | tf_op jit(solution)/shard_map/all_to_all | solution.py:110
  7.2 0.8 slice_bitcast_fusion.12
  8.0 0.8 broadcast_compare_fusion
  8.7 2.8 %bitcast_convert_fusion = f32[32,128,128]{2,1,0:T(8,128)} fusion(bf16[1,1,32,128,128]{4,3,2,1,0:T(8,128)(2,1)} %param.6), kind=kLoop, calls=%fused_computation.20 | loop fusion | flops 524288 | bytes 3145728 | tf_op jit(solution)/shard_map/convert_element_type | solution.py:25
  11.6 5.1 %all-to-all-start.1 = ((s32[8,4,2]{1,2,0:T(2,128)}), s32[8,4,2]{1,2,0:T(2,128)}, u32[]{:S(2)}, u32[]{:S(2)}) async-start(s32[8,4,2]{1,2,0:T(2,128)} %all-to-all-done), calls=%async_computation.1 | async-start | bytes 16384 | tf_op jit(solution)/shard_map/all_to_all | solution.py:109
  16.7 5.7 %all-to-all-done.1 = s32[8,4,2]{1,2,0:T(2,128)} async-done(((s32[8,4,2]{1,2,0:T(2,128)}), s32[8,4,2]{1,2,0:T(2,128)}, u32[]{:S(2)}, u32[]{:S(2)}) %all-to-all-start.1) | async-done | bytes 288 | tf_op jit(solution)/shard_map/all_to_all | solution.py:109
  22.4 4.1 %all-to-all-start.2 = ((s32[8,4,2]{1,2,0:T(2,128)}), s32[8,4,2]{1,2,0:T(2,128)S(1)}, u32[]{:S(2)}, u32[]{:S(2)}) async-start(s32[8,4,2]{1,2,0:T(2,128)} %all-to-all-done.1), calls=%async_computation.2 | async-start | bytes 16384 | tf_op jit(solution)/shard_map/all_to_all | solution.py:125
  26.5 4.7 %all-to-all-done.2 = s32[8,4,2]{1,2,0:T(2,128)S(1)} async-done(((s32[8,4,2]{1,2,0:T(2,128)}), s32[8,4,2]{1,2,0:T(2,128)S(1)}, u32[]{:S(2)}, u32[]{:S(2)}) %all-to-all-start.2) | async-done | bytes 288 | tf_op jit(solution)/shard_map/all_to_all | solution.py:125
  31.2 4.2 %all-to-all-start.3 = ((bf16[8,4,128,128]{3,2,1,0:T(8,128)(2,1)}), bf16[8,4,128,128]{3,2,1,0:T(8,128)(2,1)}, u32[]{:S(2)}, u32[]{:S(2)}) async-start(bf16[8,4,128,128]{3,2,1,0:T(8,128)(2,1)} %bitcast.11), calls=%async_computation.3 | async-start | bytes 2097152 | tf_op jit(solution)/shard_map/all_to_all | solution.py:97
  35.6 2.9 %collective-permute-start.2 = (s32[32,2]{0,1:T(2,128)S(1)}, s32[32,2]{0,1:T(2,128)S(1)}, u32[]{:S(2)}, u32[]{:S(2)}) collective-permute-start(s32[32,2]{0,1:T(2,128)S(1)} %select_select_fusion.8), channel_id=1, source_target_pairs={{0,24},{4,28},{8,0},{12,4},{16,8},{20,12},{24,16},{28,20},{1,25},{... | collective-permute-start | bytes 776 | tf_op jit(solution)/shard_map/ppermute | solution.py:11
  39.0 10.8 %collective-permute-done.2 = s32[32,2]{0,1:T(2,128)S(1)} collective-permute-done((s32[32,2]{0,1:T(2,128)S(1)}, s32[32,2]{0,1:T(2,128)S(1)}, u32[]{:S(2)}, u32[]{:S(2)}) %collective-permute-start.2) | collective-permute-done | bytes 288 | tf_op jit(solution)/shard_map/ppermute | solution.py:11
  50.5 1.9 copy.13
  52.4 1.6 collective-permute-start.3
  54.4 2.0 collective-permute-start.8
  56.4 1.5 collective-permute-start.9
  57.9 0.7 iota_reduce_fusion.7
  58.6 0.7 gather_fusion
  59.3 4.2 %all-to-all-start.4 = ((bf16[8,4,128,128]{3,2,1,0:T(8,128)(2,1)}), bf16[8,4,128,128]{3,2,1,0:T(8,128)(2,1)}, u32[]{:S(2)}, u32[]{:S(2)}) async-start(bf16[8,4,128,128]{3,2,1,0:T(8,128)(2,1)} %all-to-all-done.3), calls=%async_computation.4 | async-start | bytes 2097152 | tf_op jit(solution)/shard_map/all_to_all | solution.py:96
  63.6 0.7 iota_reduce_fusion.6
  64.3 0.7 iota_reduce_fusion.5
  65.0 23.0 %all-to-all-done.4 = bf16[8,4,128,128]{3,2,1,0:T(8,128)(2,1)} async-done(((bf16[8,4,128,128]{3,2,1,0:T(8,128)(2,1)}), bf16[8,4,128,128]{3,2,1,0:T(8,128)(2,1)}, u32[]{:S(2)}, u32[]{:S(2)}) %all-to-all-start.4) | async-done | bytes 1048608 | tf_op jit(solution)/shard_map/all_to_all | solution.py:96
  88.0 3.6 %all-to-all-start.5 = ((bf16[8,4,128,128]{3,2,1,0:T(8,128)(2,1)}), bf16[8,4,128,128]{3,2,1,0:T(8,128)(2,1)S(1)}, u32[]{:S(2)}, u32[]{:S(2)}) async-start(bf16[8,4,128,128]{3,2,1,0:T(8,128)(2,1)} %all-to-all-done.4), calls=%async_computation.5 | async-start | bytes 2097152 | tf_op jit(solution)/shard_map/all_to_all | solution.py:124
  91.6 0.7 gather_fusion.3
  92.3 1.5 collective-permute-start.12
  93.8 0.7 iota_reduce_fusion.4
  94.5 12.4 %all-to-all-done.5 = bf16[8,4,128,128]{3,2,1,0:T(8,128)(2,1)S(1)} async-done(((bf16[8,4,128,128]{3,2,1,0:T(8,128)(2,1)}), bf16[8,4,128,128]{3,2,1,0:T(8,128)(2,1)S(1)}, u32[]{:S(2)}, u32[]{:S(2)}) %all-to-all-start.5) | async-done | bytes 1048608 | tf_op jit(solution)/shard_map/all_to_all | solution.py:124
  106.9 1.2 bitcast_select_fusion
  108.1 1.6 copy.14
  109.7 2.8 %fusion.4 = bf16[32,128,128]{2,1,0:T(8,128)(2,1)} fusion(bf16[32,128,128]{2,1,0:T(8,128)(2,1)S(1)} %copy.14, f32[32,128,128]{1,2,0:T(8,128)S(1)} %copy.13, bf16[1,1,32,128,128]{4,3,2,1,0:T(8,128)(2,1)} %param.6, pred[32]{0:T(512)(128)(4,1)S(1)} %get-tuple-element.62, pred[32]{0:T(512)(128)(4,1)S(1)} %get-tuple-element.61), kind=kLoop, calls=%fused_computation.18 | loop fusion | flops 3145728 | bytes 5242944 | tf_op jit(solution)/shard_map/jit(_where)/select_n | solution.py:31
  113.1 1.5 collective-permute-start.4
  114.6 1.5 collective-permute-start.13
  116.0 0.8 iota_reduce_fusion.3
  117.5 19.1 %collective-permute-done.6 = bf16[32,128,128]{2,1,0:T(8,128)(2,1)S(1)} collective-permute-done((bf16[32,128,128]{2,1,0:T(8,128)(2,1)}, bf16[32,128,128]{2,1,0:T(8,128)(2,1)S(1)}, u32[]{:S(2)}, u32[]{:S(2)}) %collective-permute-start.6) | collective-permute-done | bytes 1048608 | tf_op jit(solution)/shard_map/ppermute | solution.py:11
  136.6 1.2 collective-permute-done.4
  137.8 1.4 broadcast_select_fusion.2
  139.7 3.0 %collective-permute-start.16 = (s32[32,2]{0,1:T(2,128)S(1)}, s32[32,2]{0,1:T(2,128)S(1)}, u32[]{:S(2)}, u32[]{:S(2)}) collective-permute-start(s32[32,2]{0,1:T(2,128)S(1)} %collective-permute-done.12), channel_id=1, source_target_pairs={{0,3},{1,0},{2,1},{3,2},{4,7},{5,4},{6,5},{7,6},{8,11},{9,8},{10,9... | collective-permute-start | bytes 776 | tf_op jit(solution)/shard_map/ppermute | solution.py:11
  142.7 1.7 collective-permute-start.7
  144.4 0.7 iota_reduce_fusion.2
  145.1 41.3 %collective-permute-done.5 = bf16[32,128,128]{2,1,0:T(8,128)(2,1)S(1)} collective-permute-done((bf16[32,128,128]{2,1,0:T(8,128)(2,1)S(1)}, bf16[32,128,128]{2,1,0:T(8,128)(2,1)S(1)}, u32[]{:S(2)}, u32[]{:S(2)}) %collective-permute-start.5) | collective-permute-done | bytes 1048608 | tf_op jit(solution)/shard_map/ppermute | solution.py:11
  186.5 1.6 collective-permute-start.10
  188.2 1.2 collective-permute-start.11
  189.4 2.3 collective-permute-start.17
  191.7 0.7 iota_reduce_fusion.1
  193.1 17.7 %collective-permute-done.10 = bf16[32,128,128]{2,1,0:T(8,128)(2,1)S(1)} collective-permute-done((bf16[32,128,128]{2,1,0:T(8,128)(2,1)S(1)}, bf16[32,128,128]{2,1,0:T(8,128)(2,1)S(1)}, u32[]{:S(2)}, u32[]{:S(2)}) %collective-permute-start.10) | collective-permute-done | bytes 1048608 | tf_op jit(solution)/shard_map/ppermute | solution.py:11
  210.9 4.0 %collective-permute-start.14 = (bf16[32,128,128]{2,1,0:T(8,128)(2,1)S(1)}, bf16[32,128,128]{2,1,0:T(8,128)(2,1)}, u32[]{:S(2)}, u32[]{:S(2)}) collective-permute-start(bf16[32,128,128]{2,1,0:T(8,128)(2,1)S(1)} %collective-permute-done.10), channel_id=1, source_target_pairs={{0,3},{1,0},{2,1},{3,2},{4,7},{5,4},{6,5},{7,6},{8,11},{9,8},{10,9... | collective-permute-start | bytes 3145736 | tf_op jit(solution)/shard_map/ppermute | solution.py:11
  214.9 1.2 collective-permute-start.15
  216.6 0.7 iota_reduce_fusion
  217.3 19.4 %collective-permute-done.14 = bf16[32,128,128]{2,1,0:T(8,128)(2,1)} collective-permute-done((bf16[32,128,128]{2,1,0:T(8,128)(2,1)S(1)}, bf16[32,128,128]{2,1,0:T(8,128)(2,1)}, u32[]{:S(2)}, u32[]{:S(2)}) %collective-permute-start.14) | collective-permute-done | bytes 1048608 | tf_op jit(solution)/shard_map/ppermute | solution.py:11
  236.7 4.4 %collective-permute-start.18 = (bf16[32,128,128]{2,1,0:T(8,128)(2,1)}, bf16[32,128,128]{2,1,0:T(8,128)(2,1)}, u32[]{:S(2)}, u32[]{:S(2)}) collective-permute-start(bf16[32,128,128]{2,1,0:T(8,128)(2,1)} %collective-permute-done.14), channel_id=1, source_target_pairs={{0,3},{1,0},{2,1},{3,2},{4,7},{5,4},{6,5},{7,6},{8,11},{9,8},{10,9... | collective-permute-start | bytes 3145736 | tf_op jit(solution)/shard_map/ppermute | solution.py:11
  241.1 1.2 collective-permute-start.19
  242.2 1.7 gather_fusion.1
  243.9 1.6 gather_fusion.2
  245.6 3.1 %fusion.10 = f32[32,128,128]{2,1,0:T(8,128)} fusion(bf16[32,128,128]{2,1,0:T(8,128)(2,1)} %gather_fusion.2, bf16[32,128,128]{2,1,0:T(8,128)(2,1)S(1)} %copy-done, pred[32]{0:T(512)(128)(4,1)S(1)} %compare_and_fusion.14, pred[32]{0:T(512)(128)(4,1)S(1)} %get-tuple-element.32, pred[32]{0:T(512)(128)(4,1)S(1)} %and.120), kind=kOutput, calls=%fused_computation.29 | convolution fusion | flops 135790592 | bytes 4194400 | tf_op jit(solution)/shard_map/uxy,uyz->uxz/dot_general | solution.py:63
  248.6 0.7 gather_fusion.4
  249.4 2.0 gather_fusion.5
  251.4 1.8 fusion.8
  253.2 2.0 gather_fusion.7
  255.2 2.0 gather_fusion.8
  257.2 1.8 fusion.6
  259.0 3.3 %collective-permute-done.18 = bf16[32,128,128]{2,1,0:T(8,128)(2,1)} collective-permute-done((bf16[32,128,128]{2,1,0:T(8,128)(2,1)}, bf16[32,128,128]{2,1,0:T(8,128)(2,1)}, u32[]{:S(2)}, u32[]{:S(2)}) %collective-permute-start.18) | collective-permute-done | bytes 1048608 | tf_op jit(solution)/shard_map/ppermute | solution.py:11
  262.2 2.0 gather_fusion.10
  264.4 2.0 gather_fusion.11
  266.4 4.5 %fusion.2 = bf16[1,1,32,128,128]{4,3,2,1,0:T(8,128)(2,1)} fusion(f32[32,128,128]{2,1,0:T(8,128)} %fusion.6, f32[32,128,128]{2,1,0:T(8,128)} %fusion.10, f32[32,128,128]{2,1,0:T(8,128)} %fusion.8, bf16[32,128,128]{2,1,0:T(8,128)(2,1)S(1)} %gather_fusion.11, bf16[32,128,128]{2,1,0:T(8,128)(2,1)S(1)} %gather_fusion.10, ...), kind=kOutput, calls=%fused_computation.16 | convolution fusion | flops 138412032 | bytes 9437312 | tf_op jit(solution)/shard_map/uxy,uyz->uxz/dot_general | solution.py:63
  (75 shorter events, 6.6 us)
Async XLA Ops:
  1.4 10.2 %all-to-all-start = ((s32[8,4,2]{1,2,0:T(2,128)}), s32[8,4,2]{1,2,0:T(2,128)}, u32[]{:S(2)}, u32[]{:S(2)}) async-start(s32[8,4,2]{1,2,0:T(2,128)} %copy.11), calls=%async_computation | async-start | bytes 16384 | tf_op jit(solution)/shard_map/all_to_all | solution.py:110
  8.7 26.8 %copy-start.1 = (s32[1,1,32,2]{2,3,1,0:T(2,128)S(1)}, s32[1,1,32,2]{2,3,1,0:T(2,128)}, u32[]{:S(2)}) copy-start(s32[1,1,32,2]{2,3,1,0:T(2,128)} %param.7) | copy-start | bytes 772
  11.6 10.8 %all-to-all-start.1 = ((s32[8,4,2]{1,2,0:T(2,128)}), s32[8,4,2]{1,2,0:T(2,128)}, u32[]{:S(2)}, u32[]{:S(2)}) async-start(s32[8,4,2]{1,2,0:T(2,128)} %all-to-all-done), calls=%async_computation.1 | async-start | bytes 16384 | tf_op jit(solution)/shard_map/all_to_all | solution.py:109
  22.4 8.8 %all-to-all-start.2 = ((s32[8,4,2]{1,2,0:T(2,128)}), s32[8,4,2]{1,2,0:T(2,128)S(1)}, u32[]{:S(2)}, u32[]{:S(2)}) async-start(s32[8,4,2]{1,2,0:T(2,128)} %all-to-all-done.1), calls=%async_computation.2 | async-start | bytes 16384 | tf_op jit(solution)/shard_map/all_to_all | solution.py:125
  31.2 28.1 %all-to-all-start.3 = ((bf16[8,4,128,128]{3,2,1,0:T(8,128)(2,1)}), bf16[8,4,128,128]{3,2,1,0:T(8,128)(2,1)}, u32[]{:S(2)}, u32[]{:S(2)}) async-start(bf16[8,4,128,128]{3,2,1,0:T(8,128)(2,1)} %bitcast.11), calls=%async_computation.3 | async-start | bytes 2097152 | tf_op jit(solution)/shard_map/all_to_all | solution.py:97
  35.6 14.3 %collective-permute-start.2 = (s32[32,2]{0,1:T(2,128)S(1)}, s32[32,2]{0,1:T(2,128)S(1)}, u32[]{:S(2)}, u32[]{:S(2)}) collective-permute-start(s32[32,2]{0,1:T(2,128)S(1)} %select_select_fusion.8), channel_id=1, source_target_pairs={{0,24},{4,28},{8,0},{12,4},{16,8},{20,12},{24,16},{28,20},{1,25},{... | collective-permute-start | bytes 776 | tf_op jit(solution)/shard_map/ppermute | solution.py:11
  38.4 11.4 %collective-permute-start = (s32[32,2]{0,1:T(2,128)S(1)}, s32[32,2]{0,1:T(2,128)S(1)}, u32[]{:S(2)}, u32[]{:S(2)}) collective-permute-start(s32[32,2]{0,1:T(2,128)S(1)} %select_select_fusion.8), channel_id=1, source_target_pairs={{0,3},{1,0},{2,1},{3,2},{4,7},{5,4},{6,5},{7,6},{8,11},{9,8},{10,9... | collective-permute-start | bytes 776 | tf_op jit(solution)/shard_map/ppermute | solution.py:11
  49.8 4.5 %collective-permute-start.1 = (s32[32,2]{0,1:T(2,128)S(1)}, s32[32,2]{0,1:T(2,128)S(1)}, u32[]{:S(2)}, u32[]{:S(2)}) collective-permute-start(s32[32,2]{0,1:T(2,128)S(1)} %get-tuple-element.57), channel_id=1, source_target_pairs={{0,2},{1,3},{2,0},{3,1},{4,6},{5,7},{6,4},{7,5},{8,10},{9,11},{10,... | collective-permute-start | bytes 776 | tf_op jit(solution)/shard_map/ppermute | solution.py:11
  52.4 3.9 %collective-permute-start.3 = (s32[32,2]{0,1:T(2,128)S(1)}, s32[32,2]{0,1:T(2,128)S(1)}, u32[]{:S(2)}, u32[]{:S(2)}) collective-permute-start(s32[32,2]{0,1:T(2,128)S(1)} %get-tuple-element.58), channel_id=1, source_target_pairs={{0,16},{4,20},{8,24},{12,28},{16,0},{20,4},{24,8},{28,12},{1,17},{... | collective-permute-start | bytes 776 | tf_op jit(solution)/shard_map/ppermute | solution.py:11
  54.4 9.9 %collective-permute-start.8 = (s32[32,2]{0,1:T(2,128)S(1)}, s32[32,2]{0,1:T(2,128)S(1)}, u32[]{:S(2)}, u32[]{:S(2)}) collective-permute-start(s32[32,2]{0,1:T(2,128)S(1)} %broadcast_select_fusion.7), channel_id=1, source_target_pairs={{0,3},{1,0},{2,1},{3,2},{4,7},{5,4},{6,5},{7,6},{8,11},{9,8},{10,9... | collective-permute-start | bytes 776 | tf_op jit(solution)/shard_map/ppermute | solution.py:11
  56.4 37.4 %collective-permute-start.9 = (s32[32,2]{0,1:T(2,128)S(1)}, s32[32,2]{0,1:T(2,128)S(1)}, u32[]{:S(2)}, u32[]{:S(2)}) collective-permute-start(s32[32,2]{0,1:T(2,128)S(1)} %broadcast_select_fusion.5), channel_id=1, source_target_pairs={{0,24},{4,28},{8,0},{12,4},{16,8},{20,12},{24,16},{28,20},{1,25},{... | collective-permute-start | bytes 776 | tf_op jit(solution)/shard_map/ppermute | solution.py:11
  59.3 28.7 %all-to-all-start.4 = ((bf16[8,4,128,128]{3,2,1,0:T(8,128)(2,1)}), bf16[8,4,128,128]{3,2,1,0:T(8,128)(2,1)}, u32[]{:S(2)}, u32[]{:S(2)}) async-start(bf16[8,4,128,128]{3,2,1,0:T(8,128)(2,1)} %all-to-all-done.3), calls=%async_computation.4 | async-start | bytes 2097152 | tf_op jit(solution)/shard_map/all_to_all | solution.py:96
  88.0 18.9 %all-to-all-start.5 = ((bf16[8,4,128,128]{3,2,1,0:T(8,128)(2,1)}), bf16[8,4,128,128]{3,2,1,0:T(8,128)(2,1)S(1)}, u32[]{:S(2)}, u32[]{:S(2)}) async-start(bf16[8,4,128,128]{3,2,1,0:T(8,128)(2,1)} %all-to-all-done.4), calls=%async_computation.5 | async-start | bytes 2097152 | tf_op jit(solution)/shard_map/all_to_all | solution.py:124
  92.3 23.7 %collective-permute-start.12 = (s32[32,2]{0,1:T(2,128)S(1)}, s32[32,2]{0,1:T(2,128)S(1)}, u32[]{:S(2)}, u32[]{:S(2)}) collective-permute-start(s32[32,2]{0,1:T(2,128)S(1)} %collective-permute-done.8), channel_id=1, source_target_pairs={{0,3},{1,0},{2,1},{3,2},{4,7},{5,4},{6,5},{7,6},{8,11},{9,8},{10,9... | collective-permute-start | bytes 776 | tf_op jit(solution)/shard_map/ppermute | solution.py:11
  112.5 24.1 %collective-permute-start.6 = (bf16[32,128,128]{2,1,0:T(8,128)(2,1)}, bf16[32,128,128]{2,1,0:T(8,128)(2,1)S(1)}, u32[]{:S(2)}, u32[]{:S(2)}) collective-permute-start(bf16[32,128,128]{2,1,0:T(8,128)(2,1)} %fusion.4), channel_id=1, source_target_pairs={{0,24},{4,28},{8,0},{12,4},{16,8},{20,12},{24,16},{28,20},{1,25},{... | collective-permute-start | bytes 3145736 | tf_op jit(solution)/shard_map/ppermute | solution.py:11
  113.1 24.8 %collective-permute-start.4 = (bf16[32,128,128]{2,1,0:T(8,128)(2,1)}, bf16[32,128,128]{2,1,0:T(8,128)(2,1)S(1)}, u32[]{:S(2)}, u32[]{:S(2)}) collective-permute-start(bf16[32,128,128]{2,1,0:T(8,128)(2,1)} %fusion.4), channel_id=1, source_target_pairs={{0,3},{1,0},{2,1},{3,2},{4,7},{5,4},{6,5},{7,6},{8,11},{9,8},{10,9... | collective-permute-start | bytes 3145736 | tf_op jit(solution)/shard_map/ppermute | solution.py:11
  114.6 29.8 %collective-permute-start.13 = (s32[32,2]{0,1:T(2,128)S(1)}, s32[32,2]{0,1:T(2,128)S(1)}, u32[]{:S(2)}, u32[]{:S(2)}) collective-permute-start(s32[32,2]{0,1:T(2,128)S(1)} %collective-permute-done.9), channel_id=1, source_target_pairs={{0,24},{4,28},{8,0},{12,4},{16,8},{20,12},{24,16},{28,20},{1,25},{... | collective-permute-start | bytes 776 | tf_op jit(solution)/shard_map/ppermute | solution.py:11
  139.3 47.1 %collective-permute-start.5 = (bf16[32,128,128]{2,1,0:T(8,128)(2,1)S(1)}, bf16[32,128,128]{2,1,0:T(8,128)(2,1)S(1)}, u32[]{:S(2)}, u32[]{:S(2)}) collective-permute-start(bf16[32,128,128]{2,1,0:T(8,128)(2,1)S(1)} %get-tuple-element.39), channel_id=1, source_target_pairs={{0,2},{1,3},{2,0},{3,1},{4,6},{5,7},{6,4},{7,5},{8,10},{9,11},{10,... | collective-permute-start | bytes 3145736 | tf_op jit(solution)/shard_map/ppermute | solution.py:11
  139.7 52.1 %collective-permute-start.16 = (s32[32,2]{0,1:T(2,128)S(1)}, s32[32,2]{0,1:T(2,128)S(1)}, u32[]{:S(2)}, u32[]{:S(2)}) collective-permute-start(s32[32,2]{0,1:T(2,128)S(1)} %collective-permute-done.12), channel_id=1, source_target_pairs={{0,3},{1,0},{2,1},{3,2},{4,7},{5,4},{6,5},{7,6},{8,11},{9,8},{10,9... | collective-permute-start | bytes 776 | tf_op jit(solution)/shard_map/ppermute | solution.py:11
  142.7 45.4 %collective-permute-start.7 = (bf16[32,128,128]{2,1,0:T(8,128)(2,1)S(1)}, bf16[32,128,128]{2,1,0:T(8,128)(2,1)S(1)}, u32[]{:S(2)}, u32[]{:S(2)}) collective-permute-start(bf16[32,128,128]{2,1,0:T(8,128)(2,1)S(1)} %get-tuple-element.40), channel_id=1, source_target_pairs={{0,16},{4,20},{8,24},{12,28},{16,0},{20,4},{24,8},{28,12},{1,17},{... | collective-permute-start | bytes 3145736 | tf_op jit(solution)/shard_map/ppermute | solution.py:11
  186.5 24.4 %collective-permute-start.10 = (bf16[32,128,128]{2,1,0:T(8,128)(2,1)S(1)}, bf16[32,128,128]{2,1,0:T(8,128)(2,1)S(1)}, u32[]{:S(2)}, u32[]{:S(2)}) collective-permute-start(bf16[32,128,128]{2,1,0:T(8,128)(2,1)S(1)} %broadcast_select_fusion.3), channel_id=1, source_target_pairs={{0,3},{1,0},{2,1},{3,2},{4,7},{5,4},{6,5},{7,6},{8,11},{9,8},{10,9... | collective-permute-start | bytes 3145736 | tf_op jit(solution)/shard_map/ppermute | solution.py:11
  188.2 26.8 %collective-permute-start.11 = (bf16[32,128,128]{2,1,0:T(8,128)(2,1)S(1)}, bf16[32,128,128]{2,1,0:T(8,128)(2,1)}, u32[]{:S(2)}, u32[]{:S(2)}) collective-permute-start(bf16[32,128,128]{2,1,0:T(8,128)(2,1)S(1)} %broadcast_select_fusion.1), channel_id=1, source_target_pairs={{0,24},{4,28},{8,0},{12,4},{16,8},{20,12},{24,16},{28,20},{1,25},{... | collective-permute-start | bytes 3145736 | tf_op jit(solution)/shard_map/ppermute | solution.py:11
  189.4 26.9 %collective-permute-start.17 = (s32[32,2]{0,1:T(2,128)S(1)}, s32[32,2]{0,1:T(2,128)S(1)}, u32[]{:S(2)}, u32[]{:S(2)}) collective-permute-start(s32[32,2]{0,1:T(2,128)S(1)} %collective-permute-done.13), channel_id=1, source_target_pairs={{0,24},{4,28},{8,0},{12,4},{16,8},{20,12},{24,16},{28,20},{1,25},{... | collective-permute-start | bytes 776 | tf_op jit(solution)/shard_map/ppermute | solution.py:11
  210.9 25.8 %collective-permute-start.14 = (bf16[32,128,128]{2,1,0:T(8,128)(2,1)S(1)}, bf16[32,128,128]{2,1,0:T(8,128)(2,1)}, u32[]{:S(2)}, u32[]{:S(2)}) collective-permute-start(bf16[32,128,128]{2,1,0:T(8,128)(2,1)S(1)} %collective-permute-done.10), channel_id=1, source_target_pairs={{0,3},{1,0},{2,1},{3,2},{4,7},{5,4},{6,5},{7,6},{8,11},{9,8},{10,9... | collective-permute-start | bytes 3145736 | tf_op jit(solution)/shard_map/ppermute | solution.py:11
  214.9 26.1 %collective-permute-start.15 = (bf16[32,128,128]{2,1,0:T(8,128)(2,1)}, bf16[32,128,128]{2,1,0:T(8,128)(2,1)}, u32[]{:S(2)}, u32[]{:S(2)}) collective-permute-start(bf16[32,128,128]{2,1,0:T(8,128)(2,1)} %collective-permute-done.11), channel_id=1, source_target_pairs={{0,24},{4,28},{8,0},{12,4},{16,8},{20,12},{24,16},{28,20},{1,25},{... | collective-permute-start | bytes 3145736 | tf_op jit(solution)/shard_map/ppermute | solution.py:11
  236.7 25.5 %collective-permute-start.18 = (bf16[32,128,128]{2,1,0:T(8,128)(2,1)}, bf16[32,128,128]{2,1,0:T(8,128)(2,1)}, u32[]{:S(2)}, u32[]{:S(2)}) collective-permute-start(bf16[32,128,128]{2,1,0:T(8,128)(2,1)} %collective-permute-done.14), channel_id=1, source_target_pairs={{0,3},{1,0},{2,1},{3,2},{4,7},{5,4},{6,5},{7,6},{8,11},{9,8},{10,9... | collective-permute-start | bytes 3145736 | tf_op jit(solution)/shard_map/ppermute | solution.py:11
  241.1 23.4 %collective-permute-start.19 = (bf16[32,128,128]{2,1,0:T(8,128)(2,1)}, bf16[32,128,128]{2,1,0:T(8,128)(2,1)}, u32[]{:S(2)}, u32[]{:S(2)}) collective-permute-start(bf16[32,128,128]{2,1,0:T(8,128)(2,1)} %collective-permute-done.15), channel_id=1, source_target_pairs={{0,24},{4,28},{8,0},{12,4},{16,8},{20,12},{24,16},{28,20},{1,25},{... | collective-permute-start | bytes 3145736 | tf_op jit(solution)/shard_map/ppermute | solution.py:11
  243.9 1.7 copy-start
where the time goes:
time: 272 us; the launch traced here: 271 us
  waiting for transfers between devices  159 us (58%)
  starting transfers between devices  61.5 us (23%)
  local copies, waits for them, and re-layouts  22.5 us (8%)
  other arithmetic  16.2 us (6%)
  matrix products  11.2 us (4%)
    ppermute x20, waiting for transfers between devices, from_behind(): lax.ppermute(value, axis, [(i, (i + by) % size) for i in range(size)])  113 us
    ppermute x20, starting transfers between devices, from_behind(): lax.ppermute(value, axis, [(i, (i + by) % size) for i in range(size)])  35.1 us
    all_to_all x1, waiting for transfers between devices, on_device(): lax.all_to_all(lax.all_to_all(own_tiles.reshape(row_count, piece_rows, ti...  23 us
    all_to_all x1, waiting for transfers between devices, on_device(): lax.all_to_all(scattered[0], 'row', split_axis=0, concat_axis=0, tiled=True)  12.4 us
    dot_general x4, matrix products, multiply(): jnp.einsum('uxy,uyz->uxz', chosen_left, chosen_right, preferred_element_t...  11.2 us
    gather x4, local copies, waits for them, and re-layouts, multiply(): chosen_right = jnp.take(right_tiles, right_slot, axis=0)  7.57 us
    gather x4, local copies, waits for them, and re-layouts, multiply(): jnp.take(left_tiles, left_slot, axis=0)  6.36 us
    all_to_all x1, waiting for transfers between devices, on_device(): lax.all_to_all(lax.all_to_all(own_index.reshape(row_count, piece_rows, 2)...  5.7 us
  transfers between devices with their start and end apart: 26, of which 13 were waited for; matrix products, arithmetic and copies ran while one was open for 16% of the time, Pallas kernels for 0%

commit v1 on v0

v1 whole, which is shorter than its diff:
```python
import functools

import jax
import jax.numpy as jnp
from jax import lax
from jax.experimental import pallas as pl
from jax.experimental.pallas import tpu as pltpu
from jax.sharding import PartitionSpec as P

STEPS = 4
VMEM_LIMIT = 48 * 1024 * 1024
AXES = ("row", "col")


def kind_of(m):
    return m % 2


def device(groups, systems, v, z, m):
    return (v * systems + m) * groups + z


def hub_pairs(groups, systems, offset):
    ring = groups - 1
    pairs = []
    for k in range(ring):
        partner = (k + offset) % ring
        if 2 * offset == ring and partner < k:
            continue
        low, high = min(k, partner), max(k, partner)
        for m in range(systems):
            if kind_of(m) == 0:
                source, target = (k, ring), (low, high)
            else:
                source, target = (0, k + 1), (low + 1, high + 1)
            pairs.append((device(groups, systems, *source, m), device(groups, systems, *target, m)))
    return pairs


def find_slots(groups, systems, own_ref, hub_refs, table, slot_ref):
    slots = slot_ref.shape[0]
    v = lax.axis_index("row") // systems
    c = lax.axis_index("col")
    kind = kind_of(lax.axis_index("row") % systems)
    first = jnp.where(kind == 0, (groups - 1) * slots, 0)
    direct = jnp.where(kind == 0, c == groups - 1, v == 0)

    @pl.when((v <= c) & direct)
    def _():
        for s in range(slots):
            slot_ref[own_ref[1 - kind, s] - first] = s

    @pl.when(v > c)
    def _():
        for s in range(slots):
            slot_ref[s] = s

    @pl.when((v <= c) & jnp.logical_not(direct))
    def _():
        key = sum(hub[kind, 0] for hub in hub_refs) // slots
        side = jnp.where(key == v, 0, 1)
        start = key * slots
        for s in range(slots):
            block = sum(hub[kind, s] for hub in hub_refs)
            table[block - start] = sum(hub[1 - kind, s] for hub in hub_refs) - first
        for s in range(slots):
            slot_ref[table[own_ref[side, s] - start]] = s


def symmetric(tile):
    wide = tile.astype(jnp.float32)
    return ((wide + wide.T) * 0.5).astype(jnp.bfloat16)


def place_of(groups, kind, v, z):
    low = groups // 2
    if kind == 0:
        return z // low, v * low + z % low
    return v // low, ((1 - z // low) * low + v % low) * low + z % low


def devices_of(groups, systems, half, m):
    found = {}
    for v in range(groups):
        for z in range(groups):
            h, p = place_of(groups, kind_of(m), v, z)
            if h == half:
                found[p] = device(groups, systems, v, z, m)
    return [found[p] for p in sorted(found)]


def half_groups(groups, systems):
    return [devices_of(groups, systems, h, m) for h in range(2) for m in range(systems)]


def larger_half(m):
    return 1 - kind_of(m)


def cross_pairs(groups, systems, larger):
    pairs = []
    for m in range(systems):
        source = larger_half(m) if larger else 1 - larger_half(m)
        pairs += list(zip(devices_of(groups, systems, source, m), devices_of(groups, systems, 1 - source, m)))
    return pairs


def sent_places(groups, larger):
    low = groups // 2
    stored = [p for p in range(low * low) if p // low <= p % low]
    return list(range(low * low)) if larger else stored


def swap_in_half(value, groups, systems):
    return lax.all_to_all(
        value,
        AXES,
        split_axis=0,
        concat_axis=0,
        axis_index_groups=half_groups(groups, systems),
        tiled=True,
    )


def stage_kernel(tiles_ref, out_ref):
    out_ref[...] = tiles_ref[...]


def sort_kernel(groups, systems, hubs, *refs):
    own_ref, hub_refs, tiles_ref = refs[0], refs[1 : 1 + hubs], refs[1 + hubs]
    out_ref, slot_ref, table = refs[2 + hubs :]
    find_slots(groups, systems, own_ref, hub_refs, table, slot_ref)
    spans, share = out_ref.shape[:2]
    for g in range(spans):
        for q in range(share):
            out_ref[g, q] = tiles_ref[slot_ref[g * share + q]]


def split_square_kernel(groups, systems, near_ref, from_larger_ref, from_smaller_ref, out_ref, dense):
    low = groups // 2
    spans, share, width = near_ref.shape[:3]
    v, z = lax.axis_index("row") // systems, lax.axis_index("col")
    kind = kind_of(lax.axis_index("row") % systems)
    half = jnp.where(kind == 0, z, v) // low

    def at(i, j=None):
        return slice(i * width, (i + 1 if j is None else j) * width)

    def square(k, h):
        larger = h == 1 - k
        far_ref = from_smaller_ref if larger else from_larger_ref
        arrived = sent_places(groups, not larger)
        for q in range(share):
            for a in range(groups):
                for b in range(a, groups):
                    side, p = place_of(groups, k, a, b)
                    if side == h:
                        tile = near_ref[p, q]
                    elif p < spans // 2:
                        tile = far_ref[arrived.index(p), q]
                    else:
                        continue
                    if a == b:
                        dense[q, at(a), at(a)] = symmetric(tile)
                    else:
                        dense[q, at(a), at(b)] = tile
                        dense[q, at(b), at(a)] = tile.T
            if k == 0:
                rows, columns = (0, (h + 1) * low), (h * low, (h + 1) * low)
            else:
                rows, columns = (h * low, (h + 1) * low), (h * low, groups)
            product = jnp.dot(
                dense[q, at(*rows), :], dense[q, :, at(*columns)], preferred_element_type=jnp.float32
            ).astype(jnp.bfloat16)
            for a in range(*rows):
                for b in range(max(a, columns[0]), columns[1]):
                    out_ref[place_of(groups, k, a, b)[1], q] = product[at(a - rows[0]), at(b - columns[0])]

    for k in range(min(systems, 2)):
        for h in range(2):
            pl.when((kind == k) & (half == h))(functools.partial(square, k, h))


def unsort_kernel(systems, slot_ref, sorted_ref, out_ref):
    spans, share = sorted_ref.shape[:2]
    stored = lax.axis_index("row") // systems <= lax.axis_index("col")

    @pl.when(stored)
    def _():
        for g in range(spans):
            for q in range(share):
                out_ref[slot_ref[g * share + q]] = sorted_ref[g, q]

    @pl.when(jnp.logical_not(stored))
    def _():
        out_ref[...] = jnp.zeros_like(out_ref)


def split_plan(own_tiles, own_index, hubs, groups, systems):
    slots, width = own_tiles.shape[0], own_tiles.shape[1]
    spans = groups * groups // 2
    share = slots // spans
    smem = pl.BlockSpec(memory_space=pltpu.SMEM)
    vmem = pl.BlockSpec(memory_space=pltpu.VMEM)
    params = pltpu.CompilerParams(vmem_limit_bytes=VMEM_LIMIT)
    region = jax.ShapeDtypeStruct(own_tiles.shape, jnp.bfloat16)
    by_group = jax.ShapeDtypeStruct((spans, share, width, width), jnp.bfloat16)

    staged = pl.pallas_call(
        stage_kernel,
        out_shape=region,
        in_specs=[vmem],
        out_specs=vmem,
        compiler_params=params,
        cost_estimate=pl.CostEstimate(flops=0, bytes_accessed=4 * own_tiles.size, transcendentals=0),
        name="stage_tiles",
    )(own_tiles)

    by_label, slot = pl.pallas_call(
        functools.partial(sort_kernel, groups, systems, len(hubs)),
        out_shape=[by_group, jax.ShapeDtypeStruct((slots,), jnp.int32)],
        in_specs=[smem] * (1 + len(hubs)) + [vmem],
        out_specs=[vmem, smem],
        scratch_shapes=[pltpu.SMEM((slots,), jnp.int32)],
        compiler_params=params,
        name="sort_by_chain",
    )(own_index, *hubs, staged)

    near = swap_in_half(by_label, groups, systems)
    crossing = []
    for larger in (True, False):
        sent = jnp.concatenate([near[p : p + 1] for p in sent_places(groups, larger)])
        crossing.append(lax.ppermute(sent, AXES, cross_pairs(groups, systems, larger)))
    squares = pl.pallas_call(
        functools.partial(split_square_kernel, groups, systems),
        out_shape=by_group,
        in_specs=[vmem] * 3,
        out_specs=vmem,
        scratch_shapes=[pltpu.VMEM((share, groups * width, groups * width), jnp.bfloat16)],
        compiler_params=params,
        name="square_chains",
    )(near, *crossing)
    returned = swap_in_half(squares, groups, systems)

    return pl.pallas_call(
        functools.partial(unsort_kernel, systems),
        out_shape=region,
        in_specs=[smem, vmem],
        out_specs=vmem,
        compiler_params=params,
        name="back_to_slots",
    )(slot, returned)


def spread_sort_kernel(groups, systems, hubs, *refs):
    own_ref, hub_refs, tiles_ref = refs[0], refs[1 : 1 + hubs], refs[1 + hubs]
    sorted_ref, slot_ref, table = refs[2 + hubs :]
    slots = slot_ref.shape[0]
    find_slots(groups, systems, own_ref, hub_refs, table, slot_ref)

    def move(t, carry):
        sorted_ref[t] = tiles_ref[slot_ref[t]]
        return carry

    lax.fori_loop(0, slots, move, 0)


def spread_unsort_kernel(slot_ref, sorted_ref, out_ref):
    def move(t, carry):
        out_ref[slot_ref[t]] = sorted_ref[t]
        return carry

    lax.fori_loop(0, out_ref.shape[0], move, 0)


def spread_square_kernel(groups, systems, tiles_ref, out_ref, dense):
    per_owner, width = tiles_ref.shape[1], tiles_ref.shape[2]

    def piece(v, m, c):
        return (v * systems + m) * groups + c

    def at(i):
        return pl.ds(i * width if isinstance(i, int) else pl.multiple_of(i * width, width), width)

    def one_chain(m, q):
        for i in range(groups):
            dense[at(i), at(i)] = symmetric(tiles_ref[piece(i, m, i), q])
            for j in range(i + 1, groups):
                tile = tiles_ref[piece(i, m, j), q]
                dense[at(i), at(j)] = tile
                dense[at(j), at(i)] = tile.T

        def one_tile(p, carry):
            a, b = p // groups, p % groups
            total = jnp.zeros((width, width), jnp.float32)
            for s in range(STEPS):
                k = lax.rem(a + b + s, groups)
                total += jnp.dot(dense[at(a), at(k)], dense[at(k), at(b)], preferred_element_type=jnp.float32)
            out_ref[piece(a, m, b), q] = jnp.where(a <= b, total, 0.0).astype(jnp.bfloat16)
            return carry

        lax.fori_loop(0, groups * groups, one_tile, 0)

    for m in range(systems):
        for q in range(per_owner):
            one_chain(m, q)


def spread_plan(own_tiles, own_index, hubs, groups, systems):
    slots, width = own_tiles.shape[0], own_tiles.shape[1]
    devices = groups * groups * systems
    per_owner = -(-slots // devices)
    pieces = per_owner * devices
    smem = pl.BlockSpec(memory_space=pltpu.SMEM)
    vmem = pl.BlockSpec(memory_space=pltpu.VMEM)
    params = pltpu.CompilerParams(vmem_limit_bytes=VMEM_LIMIT)

    by_label, slot = pl.pallas_call(
        functools.partial(spread_sort_kernel, groups, systems, len(hubs)),
        out_shape=(
            jax.ShapeDtypeStruct((slots, width, width), jnp.bfloat16),
            jax.ShapeDtypeStruct((slots,), jnp.int32),
        ),
        in_specs=[smem] * (1 + len(hubs)) + [vmem],
        out_specs=(vmem, smem),
        scratch_shapes=[pltpu.SMEM((slots,), jnp.int32)],
        compiler_params=params,
        name="sort_by_chain",
    )(own_index, *hubs, own_tiles)

    if pieces > slots:
        by_label = jnp.concatenate([by_label, jnp.zeros((pieces - slots, width, width), jnp.bfloat16)])
    outgoing = by_label.reshape(devices, per_owner, width, width)
    chains = lax.all_to_all(outgoing, AXES, split_axis=0, concat_axis=0, tiled=True)
    squares = pl.pallas_call(
        functools.partial(spread_square_kernel, groups, systems),
        out_shape=jax.ShapeDtypeStruct(chains.shape, jnp.bfloat16),
        in_specs=[vmem],
        out_specs=vmem,
        scratch_shapes=[pltpu.VMEM((groups * width, groups * width), jnp.bfloat16)],
        compiler_params=params,
        name="square_chains",
    )(chains)
    returned = lax.all_to_all(squares, AXES, split_axis=0, concat_axis=0, tiled=True)

    return pl.pallas_call(
        spread_unsort_kernel,
        out_shape=jax.ShapeDtypeStruct((slots, width, width), jnp.bfloat16),
        in_specs=[smem, vmem],
        out_specs=vmem,
        compiler_params=params,
        name="back_to_slots",
    )(slot, returned.reshape(pieces, width, width)[:slots])


def on_device(block_tiles, block_index):
    groups = lax.axis_size("col")
    systems = lax.axis_size("row") // groups
    own_tiles = block_tiles[0, 0]
    own_index = block_index[0, 0].T
    slots = own_tiles.shape[0]
    spans = groups * groups // 2

    hubs = [lax.ppermute(own_index, AXES, hub_pairs(groups, systems, offset)) for offset in reversed(range((groups + 1) // 2))]
    whole_window = groups == STEPS and slots % spans == 0
    plan = split_plan if whole_window else spread_plan
    return plan(own_tiles, own_index, hubs, groups, systems)[None, None]


def solution(mesh):
    in_specs = (P("row", "col", None, None, None), P("row", "col", None, None))
    out_specs = P("row", "col", None, None, None)
    return jax.shard_map(
        on_device, mesh=mesh, in_specs=in_specs, out_specs=out_specs, check_vma=False
    )
```

time: 272 us -> 65.7 us (0.24)
  waiting for transfers between devices: 159 us -> 13.6 us
  starting transfers between devices: 61.5 us -> 8.73 us
  blocking collectives: 0 us -> 37.2 us
  local copies, waits for them, and re-layouts: 22.5 us -> 1.97 us
  other arithmetic: 16.2 us -> 0.04 us
  matrix products: 11.2 us -> 0 us
  Pallas kernels: 0 us -> 3.75 us
    ppermute x20 -> x4, waiting for transfers between devices: 113 us -> 13.6 us  [the longest x2 9.02 us: split_plan(): lax.ppermute(sent, AXES, cross_pairs(groups, systems, larger))]
    all_to_all x6 -> x0, waiting for transfers between devices: 45.8 us -> none  [the longest x1 23 us: on_device(): lax.all_to_all(lax.all_to_all(own_tiles.reshape(row_count, piece_rows, ti...]
    all_to_all x0 -> x2, blocking collectives: none -> 37.2 us  [swap_in_half(): lax.all_to_all(value, AXES, split_axis=0, concat_axis=0, axis_index_group...]
    all_to_all x6 -> x0, starting transfers between devices: 26.4 us -> none  [the longest x1 5.17 us: on_device(): lax.all_to_all(own_index.reshape(row_count, piece_rows, 2), 'row', split_...]
    ppermute x20 -> x4, starting transfers between devices: 35.1 us -> 8.73 us  [the longest x2 6.79 us: split_plan(): lax.ppermute(sent, AXES, cross_pairs(groups, systems, larger))]
    gather x12 -> x0, local copies, waits for them, and re-layouts: 16.7 us -> none  [the longest x4 7.57 us: multiply(): chosen_right = jnp.take(right_tiles, right_slot, axis=0)]
    dot_general x4 -> x0, matrix products: 11.2 us -> none  [multiply(): jnp.einsum('uxy,uyz->uxz', chosen_left, chosen_right, preferred_element_t...]
    select_n x21 -> x0, other arithmetic: 5.7 us -> none  [the longest x1 2.79 us: assemble(): jnp.where(own_valid[:, None, None], own_kept, jnp.where(mirror_valid[:, N...]
  transfers between devices with their start and end apart: 26 -> 4, of which waited for: 13 -> 3; matrix products, arithmetic and copies ran while one was open for 16% -> 0% of each run, Pallas kernels for 0% -> 0%
where the time goes in v1:
time: 65.7 us; the launch traced here: 65.4 us
  blocking collectives  37.2 us (57%)
  waiting for transfers between devices  13.6 us (21%)
  starting transfers between devices  8.73 us (13%)
  Pallas kernels  3.75 us (6%)
  local copies, waits for them, and re-layouts  1.97 us (3%)
    all_to_all x2, blocking collectives, swap_in_half(): lax.all_to_all(value, AXES, split_axis=0, concat_axis=0, axis_index_group...  37.2 us
    ppermute x2, waiting for transfers between devices, split_plan(): lax.ppermute(sent, AXES, cross_pairs(groups, systems, larger))  9.02 us
    ppermute x2, starting transfers between devices, split_plan(): lax.ppermute(sent, AXES, cross_pairs(groups, systems, larger))  6.79 us
    ppermute x2, waiting for transfers between devices, on_device(): lax.ppermute(own_index, AXES, hub_pairs(groups, systems, offset))  4.61 us
    ppermute x2, starting transfers between devices, on_device(): lax.ppermute(own_index, AXES, hub_pairs(groups, systems, offset))  1.94 us
    unnamed x4, local copies, waits for them, and re-layouts  1.9 us
    pallas_call x1, Pallas kernels, split_plan(): pl.pallas_call(functools.partial(unsort_kernel, systems), out_shape=regio...  1.6 us
    pallas_call x1, Pallas kernels, split_plan(): pl.pallas_call(functools.partial(sort_kernel, groups, systems, len(hubs))...  1.42 us
  transfers between devices with their start and end apart: 4, of which 3 were waited for; matrix products, arithmetic and copies ran while one was open for 0% of the time, Pallas kernels for 0%

profile of v1, /device:TPU:0, one launch (start us, length us, event | category | flops | bytes accessed | tf_op | source)
XLA Modules:
  0.0 65.4 jit_solution(15917117535294583832)
XLA Ops:
  0.0 0.0 copy-start.1
  0.0 0.7 %copy-done.1 = s32[1,1,32,2]{2,3,1,0:T(2,128)S(1)} copy-done((s32[1,1,32,2]{2,3,1,0:T(2,128)S(1)}, s32[1,1,32,2]{2,3,1,0:T(2,128)}, u32[]{:S(2)}) %copy-start.1) | copy-done | bytes 280
  0.7 1.3 %collective-permute-start.1 = (s32[2,32]{1,0:T(2,128)S(1)}, s32[2,32]{1,0:T(2,128)S(1)}, u32[]{:S(2)}, u32[]{:S(2)}) collective-permute-start(s32[2,32]{1,0:T(2,128)S(1)} %bitcast.6), channel_id=1, source_target_pairs={{3,0},{5,13},{11,9},{6,22},{19,18},{7,31}} | collective-permute-start | bytes 776 | tf_op jit(solution)/shard_map/ppermute | solution.py:364
  2.0 0.7 %collective-permute-start = (s32[2,32]{1,0:T(2,128)S(1)}, s32[2,32]{1,0:T(2,128)S(1)}, u32[]{:S(2)}, u32[]{:S(2)}) collective-permute-start(s32[2,32]{1,0:T(2,128)S(1)} %bitcast.7), channel_id=1, source_target_pairs={{3,1},{5,14},{11,10},{6,23},{19,2},{7,15}} | collective-permute-start | bytes 776 | tf_op jit(solution)/shard_map/ppermute | solution.py:364
  2.6 0.0 copy-start
  2.6 1.2 %copy-done = bf16[1,1,32,128,128]{4,3,2,1,0:T(8,128)(2,1)S(1)} copy-done((bf16[1,1,32,128,128]{4,3,2,1,0:T(8,128)(2,1)S(1)}, bf16[1,1,32,128,128]{4,3,2,1,0:T(8,128)(2,1)}, u32[]{:S(2)}) %copy-start) | copy-done | bytes 1048600
  3.9 0.1 stage_tiles.1.refs_3_
  3.9 4.6 %collective-permute-done.1.refs_2_ = s32[2,32]{1,0:T(2,128)S(1)} collective-permute-done((s32[2,32]{1,0:T(2,128)S(1)}, s32[2,32]{1,0:T(2,128)S(1)}, u32[]{:S(2)}, u32[]{:S(2)}) %collective-permute-start.1) | collective-permute-done | bytes 288 | tf_op jit(solution)/shard_map/ppermute | solution.py:364
  8.5 0.0 collective-permute-done.refs_1_
  8.5 1.4 %sort_by_chain.1 = (bf16[8,4,128,128]{3,2,1,0:T(8,128)(2,1)S(1)}, s32[32]{0:T(128)S(1)}) custom-call(s32[2,32]{1,0:T(2,128)S(1)} %bitcast.8, s32[2,32]{1,0:T(2,128)S(1)} %collective-permute-done.refs_1_, s32[2,32]{1,0:T(2,128)S(1)} %collective-permute-done.1.refs_2_, bf16[32,128,128]{2,1,0:T(8,128)(2,1)S(1)} %stage_tiles.1.refs_3_), custom_call_target="tpu_custom_call" | custom-call | tf_op jit(solution)/shard_map/sort_by_chain/pallas_call | solution.py:219
  10.0 21.5 %all_to_all.10.near_ref = bf16[8,4,128,128]{3,2,1,0:T(8,128)(2,1)S(1)} all-to-all(bf16[8,4,128,128]{3,2,1,0:T(8,128)(2,1)S(1)} %get-tuple-element.8), channel_id=1, replica_groups={{0,1,8,9,16,17,24,25},{6,7,14,15,4,5,12,13},{2,3,10,11,18,19,26,27},{22..., dimensions={0} | all-to-all | bytes 2097152 | tf_op jit(solution)/shard_map/all_to_all | solution.py:115
  31.5 1.3 %collective-permute-start.2 = (bf16[4,4,128,128]{3,2,1,0:T(8,128)(2,1)S(1)}, bf16[4,4,128,128]{3,2,1,0:T(8,128)(2,1)S(1)}, u32[]{:S(2)}, u32[]{:S(2)}) collective-permute-start(bf16[4,4,128,128]{3,2,1,0:T(8,128)(2,1)S(1)} %slice.18), channel_id=1, source_target_pairs={{2,0},{3,1},{10,8},{11,9},{18,16},{19,17},{26,24},{27,25},{6,22},{... | collective-permute-start | bytes 1572872 | tf_op jit(solution)/shard_map/ppermute | solution.py:233
  32.9 5.5 %collective-permute-start.3 = (bf16[3,4,128,128]{3,2,1,0:T(8,128)(2,1)S(1)}, bf16[3,4,128,128]{3,2,1,0:T(8,128)(2,1)S(1)}, u32[]{:S(2)}, u32[]{:S(2)}) collective-permute-start(bf16[3,4,128,128]{3,2,1,0:T(8,128)(2,1)S(1)} %pad_maximum_fusion), channel_id=1, source_target_pairs={{0,2},{1,3},{8,10},{9,11},{16,18},{17,19},{24,26},{25,27},{22,6},{... | collective-permute-start | bytes 1179656 | tf_op jit(solution)/shard_map/ppermute | solution.py:233
  38.4 5.3 %collective-permute-done.3.from_smaller_ref = bf16[3,4,128,128]{3,2,1,0:T(8,128)(2,1)S(1)} collective-permute-done((bf16[3,4,128,128]{3,2,1,0:T(8,128)(2,1)S(1)}, bf16[3,4,128,128]{3,2,1,0:T(8,128)(2,1)S(1)}, u32[]{:S(2)}, u32[]{:S(2)}) %collective-permute-start.3) | collective-permute-done | bytes 393248 | tf_op jit(solution)/shard_map/ppermute | solution.py:233
  43.7 3.7 %collective-permute-done.2.from_larger_ref = bf16[4,4,128,128]{3,2,1,0:T(8,128)(2,1)S(1)} collective-permute-done((bf16[4,4,128,128]{3,2,1,0:T(8,128)(2,1)S(1)}, bf16[4,4,128,128]{3,2,1,0:T(8,128)(2,1)S(1)}, u32[]{:S(2)}, u32[]{:S(2)}) %collective-permute-start.2) | collective-permute-done | bytes 524320 | tf_op jit(solution)/shard_map/ppermute | solution.py:233
  47.4 0.7 square_chains.1
  48.1 15.7 %all_to_all.11.sorted_ref = bf16[8,4,128,128]{3,2,1,0:T(8,128)(2,1)S(1)} all-to-all(bf16[8,4,128,128]{3,2,1,0:T(8,128)(2,1)S(1)} %square_chains.1), channel_id=1, replica_groups={{0,1,8,9,16,17,24,25},{6,7,14,15,4,5,12,13},{2,3,10,11,18,19,26,27},{22..., dimensions={0} | all-to-all | bytes 2097152 | tf_op jit(solution)/shard_map/all_to_all | solution.py:115
  63.8 1.6 %back_to_slots.1 = bf16[32,128,128]{2,1,0:T(8,128)(2,1)} custom-call(s32[32]{0:T(128)S(1)} %get-tuple-element.7.slot_ref, bf16[8,4,128,128]{3,2,1,0:T(8,128)(2,1)S(1)} %all_to_all.11.sorted_ref), custom_call_target="tpu_custom_call" | custom-call | tf_op jit(solution)/shard_map/back_to_slots/pallas_call | solution.py:245
  (4 shorter events, 0.1 us)
Async XLA Ops:
  0.0 0.7 %copy-start.1 = (s32[1,1,32,2]{2,3,1,0:T(2,128)S(1)}, s32[1,1,32,2]{2,3,1,0:T(2,128)}, u32[]{:S(2)}) copy-start(s32[1,1,32,2]{2,3,1,0:T(2,128)} %param.3) | copy-start | bytes 772
  0.7 7.9 %collective-permute-start.1 = (s32[2,32]{1,0:T(2,128)S(1)}, s32[2,32]{1,0:T(2,128)S(1)}, u32[]{:S(2)}, u32[]{:S(2)}) collective-permute-start(s32[2,32]{1,0:T(2,128)S(1)} %bitcast.6), channel_id=1, source_target_pairs={{3,0},{5,13},{11,9},{6,22},{19,18},{7,31}} | collective-permute-start | bytes 776 | tf_op jit(solution)/shard_map/ppermute | solution.py:364
  2.0 6.6 %collective-permute-start = (s32[2,32]{1,0:T(2,128)S(1)}, s32[2,32]{1,0:T(2,128)S(1)}, u32[]{:S(2)}, u32[]{:S(2)}) collective-permute-start(s32[2,32]{1,0:T(2,128)S(1)} %bitcast.7), channel_id=1, source_target_pairs={{3,1},{5,14},{11,10},{6,23},{19,2},{7,15}} | collective-permute-start | bytes 776 | tf_op jit(solution)/shard_map/ppermute | solution.py:364
  2.6 1.2 %copy-start = (bf16[1,1,32,128,128]{4,3,2,1,0:T(8,128)(2,1)S(1)}, bf16[1,1,32,128,128]{4,3,2,1,0:T(8,128)(2,1)}, u32[]{:S(2)}) copy-start(bf16[1,1,32,128,128]{4,3,2,1,0:T(8,128)(2,1)} %param.2) | copy-start | bytes 3145732
  31.5 15.9 %collective-permute-start.2 = (bf16[4,4,128,128]{3,2,1,0:T(8,128)(2,1)S(1)}, bf16[4,4,128,128]{3,2,1,0:T(8,128)(2,1)S(1)}, u32[]{:S(2)}, u32[]{:S(2)}) collective-permute-start(bf16[4,4,128,128]{3,2,1,0:T(8,128)(2,1)S(1)} %slice.18), channel_id=1, source_target_pairs={{2,0},{3,1},{10,8},{11,9},{18,16},{19,17},{26,24},{27,25},{6,22},{... | collective-permute-start | bytes 1572872 | tf_op jit(solution)/shard_map/ppermute | solution.py:233
  32.9 10.8 %collective-permute-start.3 = (bf16[3,4,128,128]{3,2,1,0:T(8,128)(2,1)S(1)}, bf16[3,4,128,128]{3,2,1,0:T(8,128)(2,1)S(1)}, u32[]{:S(2)}, u32[]{:S(2)}) collective-permute-start(bf16[3,4,128,128]{3,2,1,0:T(8,128)(2,1)S(1)} %pad_maximum_fusion), channel_id=1, source_target_pairs={{0,2},{1,3},{8,10},{9,11},{16,18},{17,19},{24,26},{25,27},{22,6},{... | collective-permute-start | bytes 1179656 | tf_op jit(solution)/shard_map/ppermute | solution.py:233

commit v2 on v1

--- a/solution.py
+++ b/solution.py
@@ -74,9 +74,7 @@
 
 def place_of(groups, kind, v, z):
     low = groups // 2
-    if kind == 0:
-        return z // low, v * low + z % low
-    return v // low, ((1 - z // low) * low + v % low) * low + z % low
+    return (z // low, v * low + z % low) if kind == 0 else (v // low, z * low + v % low)
 
 
 def devices_of(groups, systems, half, m):
@@ -93,33 +91,36 @@
     return [devices_of(groups, systems, h, m) for h in range(2) for m in range(systems)]
 
 
-def larger_half(m):
-    return 1 - kind_of(m)
-
-
-def cross_pairs(groups, systems, larger):
+def line_groups(groups, systems):
+    lines = []
+    for m in range(systems):
+        for fixed in range(groups):
+            line = [(i, fixed) if kind_of(m) == 0 else (fixed, i) for i in range(groups)]
+            lines.append([device(groups, systems, v, z, m) for v, z in line])
+    return lines
+
+
+def move_pairs(groups, systems, offset):
     pairs = []
     for m in range(systems):
-        source = larger_half(m) if larger else 1 - larger_half(m)
-        pairs += list(zip(devices_of(groups, systems, source, m), devices_of(groups, systems, 1 - source, m)))
+        for v in range(groups):
+            for z in range(groups):
+                target = (v, z ^ offset) if kind_of(m) == 0 else (v ^ offset, z)
+                pairs.append((device(groups, systems, v, z, m), device(groups, systems, *target, m)))
     return pairs
 
 
-def sent_places(groups, larger):
-    low = groups // 2
-    stored = [p for p in range(low * low) if p // low <= p % low]
-    return list(range(low * low)) if larger else stored
-
-
-def swap_in_half(value, groups, systems):
-    return lax.all_to_all(
-        value,
+def swap(value, owners, members):
+    shape = value.shape
+    arrived = lax.all_to_all(
+        value.reshape(owners, -1, *shape[1:]),
         AXES,
         split_axis=0,
         concat_axis=0,
-        axis_index_groups=half_groups(groups, systems),
+        axis_index_groups=members,
         tiled=True,
     )
+    return arrived.reshape(shape)
 
 
 def stage_kernel(tiles_ref, out_ref):
@@ -130,35 +131,53 @@
     own_ref, hub_refs, tiles_ref = refs[0], refs[1 : 1 + hubs], refs[1 + hubs]
     out_ref, slot_ref, table = refs[2 + hubs :]
     find_slots(groups, systems, own_ref, hub_refs, table, slot_ref)
-    spans, share = out_ref.shape[:2]
-    for g in range(spans):
-        for q in range(share):
-            out_ref[g, q] = tiles_ref[slot_ref[g * share + q]]
-
-
-def split_square_kernel(groups, systems, near_ref, from_larger_ref, from_smaller_ref, out_ref, dense):
+    for label in range(slot_ref.shape[0]):
+        out_ref[label] = tiles_ref[slot_ref[label]]
+
+
+def pick_kernel(groups, systems, near_ref, next_ref, far_ref, far_next_ref):
     low = groups // 2
-    spans, share, width = near_ref.shape[:3]
+    share = far_ref.shape[0] // low
+    kind = kind_of(lax.axis_index("row") % systems)
+    mine = lax.rem(jnp.where(kind == 0, lax.axis_index("col"), lax.axis_index("row") // systems), low)
+    for source in range(groups):
+        next_ref[source * share : (source + 1) * share] = near_ref[pl.ds((source * low + 1 - mine) * share, share)]
+    for i in range(low):
+        source = i + kind * low
+        here = slice(i * share, (i + 1) * share)
+        far_ref[here] = near_ref[pl.ds((source * low + mine) * share, share)]
+        far_next_ref[here] = near_ref[pl.ds((source * low + 1 - mine) * share, share)]
+
+
+def split_square_kernel(groups, systems, near_ref, next_ref, far_ref, far_next_ref, out_ref, dense):
+    low = groups // 2
+    spans = groups * low
+    share, width = near_ref.shape[0] // spans, near_ref.shape[1]
     v, z = lax.axis_index("row") // systems, lax.axis_index("col")
     kind = kind_of(lax.axis_index("row") % systems)
-    half = jnp.where(kind == 0, z, v) // low
+    line = jnp.where(kind == 0, z, v)
+    half, mine = line // low, lax.rem(line, low)
 
     def at(i, j=None):
         return slice(i * width, (i + 1 if j is None else j) * width)
 
+    def tile_of(k, h, a, b, q):
+        source, across = (a, b) if k == 0 else (b, a)
+        if across // low == h:
+            ours, theirs = near_ref[(source * low + mine) * share + q], next_ref[source * share + q]
+        elif source // low == k:
+            here = (source - k * low) * share + q
+            ours, theirs = far_ref[here], far_next_ref[here]
+        else:
+            return None
+        return jnp.where(mine == across % low, ours, theirs)
+
     def square(k, h):
-        larger = h == 1 - k
-        far_ref = from_smaller_ref if larger else from_larger_ref
-        arrived = sent_places(groups, not larger)
         for q in range(share):
             for a in range(groups):
                 for b in range(a, groups):
-                    side, p = place_of(groups, k, a, b)
-                    if side == h:
-                        tile = near_ref[p, q]
-                    elif p < spans // 2:
-                        tile = far_ref[arrived.index(p), q]
-                    else:
+                    tile = tile_of(k, h, a, b, q)
+                    if tile is None:
                         continue
                     if a == b:
                         dense[q, at(a), at(a)] = symmetric(tile)
@@ -174,22 +193,21 @@
             ).astype(jnp.bfloat16)
             for a in range(*rows):
                 for b in range(max(a, columns[0]), columns[1]):
-                    out_ref[place_of(groups, k, a, b)[1], q] = product[at(a - rows[0]), at(b - columns[0])]
-
-    for k in range(min(systems, 2)):
+                    place = place_of(groups, k, a, b)[1]
+                    out_ref[place * share + q] = product[at(a - rows[0]), at(b - columns[0])]
+
+    for k in sorted({kind_of(m) for m in range(systems)}):
         for h in range(2):
             pl.when((kind == k) & (half == h))(functools.partial(square, k, h))
 
 
 def unsort_kernel(systems, slot_ref, sorted_ref, out_ref):
-    spans, share = sorted_ref.shape[:2]
     stored = lax.axis_index("row") // systems <= lax.axis_index("col")
 
     @pl.when(stored)
     def _():
-        for g in range(spans):
-            for q in range(share):
-                out_ref[slot_ref[g * share + q]] = sorted_ref[g, q]
+        for label in range(slot_ref.shape[0]):
+            out_ref[slot_ref[label]] = sorted_ref[label]
 
     @pl.when(jnp.logical_not(stored))
     def _():
@@ -198,17 +216,19 @@
 
 def split_plan(own_tiles, own_index, hubs, groups, systems):
     slots, width = own_tiles.shape[0], own_tiles.shape[1]
-    spans = groups * groups // 2
+    low = groups // 2
+    spans = groups * low
     share = slots // spans
     smem = pl.BlockSpec(memory_space=pltpu.SMEM)
     vmem = pl.BlockSpec(memory_space=pltpu.VMEM)
     params = pltpu.CompilerParams(vmem_limit_bytes=VMEM_LIMIT)
-    region = jax.ShapeDtypeStruct(own_tiles.shape, jnp.bfloat16)
-    by_group = jax.ShapeDtypeStruct((spans, share, width, width), jnp.bfloat16)
+
+    def tiles(count):
+        return jax.ShapeDtypeStruct((count, width, width), jnp.bfloat16)
 
     staged = pl.pallas_call(
         stage_kernel,
-        out_shape=region,
+        out_shape=tiles(slots),
         in_specs=[vmem],
         out_specs=vmem,
         compiler_params=params,
@@ -218,7 +238,7 @@
 
     by_label, slot = pl.pallas_call(
         functools.partial(sort_kernel, groups, systems, len(hubs)),
-        out_shape=[by_group, jax.ShapeDtypeStruct((slots,), jnp.int32)],
+        out_shape=[tiles(slots), jax.ShapeDtypeStruct((slots,), jnp.int32)],
         in_specs=[smem] * (1 + len(hubs)) + [vmem],
         out_specs=[vmem, smem],
         scratch_shapes=[pltpu.SMEM((slots,), jnp.int32)],
@@ -226,25 +246,33 @@
         name="sort_by_chain",
     )(own_index, *hubs, staged)
 
-    near = swap_in_half(by_label, groups, systems)
-    crossing = []
-    for larger in (True, False):
-        sent = jnp.concatenate([near[p : p + 1] for p in sent_places(groups, larger)])
-        crossing.append(lax.ppermute(sent, AXES, cross_pairs(groups, systems, larger)))
+    near = swap(by_label, groups, line_groups(groups, systems))
+    moves = pl.pallas_call(
+        functools.partial(pick_kernel, groups, systems),
+        out_shape=[tiles(groups * share), tiles(low * share), tiles(low * share)],
+        in_specs=[vmem],
+        out_specs=[vmem] * 3,
+        compiler_params=params,
+        name="pick_moves",
+    )(near)
+    moved = [
+        lax.ppermute(move, AXES, move_pairs(groups, systems, offset))
+        for move, offset in zip(moves, (1, low, low + 1))
+    ]
     squares = pl.pallas_call(
         functools.partial(split_square_kernel, groups, systems),
-        out_shape=by_group,
-        in_specs=[vmem] * 3,
+        out_shape=tiles(slots),
+        in_specs=[vmem] * 4,
         out_specs=vmem,
         scratch_shapes=[pltpu.VMEM((share, groups * width, groups * width), jnp.bfloat16)],
         compiler_params=params,
         name="square_chains",
-    )(near, *crossing)
-    returned = swap_in_half(squares, groups, systems)
+    )(near, *moved)
+    returned = swap(squares, spans, half_groups(groups, systems))
 
     return pl.pallas_call(
         functools.partial(unsort_kernel, systems),
-        out_shape=region,
+        out_shape=tiles(slots),
         in_specs=[smem, vmem],
         out_specs=vmem,
         compiler_params=params,

time: 65.7 us -> 64.5 us (0.982)
  blocking collectives: 37.2 us -> 33 us
  waiting for transfers between devices: 13.6 us -> 17.4 us
  starting transfers between devices: 8.73 us -> 7.35 us
    all_to_all x2, blocking collectives: 37.2 us -> 33 us  [swap(): lax.all_to_all(value.reshape(owners, -1, *shape[1:]), AXES, split_axis=0,...]
    ppermute x2 -> x3, waiting for transfers between devices: 9.02 us -> 12.8 us  [split_plan(): lax.ppermute(move, AXES, move_pairs(groups, systems, offset))]
    ppermute x2 -> x3, starting transfers between devices: 6.79 us -> 5.41 us  [split_plan(): lax.ppermute(move, AXES, move_pairs(groups, systems, offset))]
    pallas_call x2 -> x3, Pallas kernels: 1.67 us -> 1.74 us  [the longest x1 1.6 us: split_plan(): pl.pallas_call(functools.partial(unsort_kernel, systems), out_shape=tiles...]
  transfers between devices with their start and end apart: 4 -> 5, of which waited for: 3 -> 3; matrix products, arithmetic and copies ran while one was open for 0% -> 0% of each run, Pallas kernels for 0% -> 0%
where the time goes in v2:
time: 64.5 us; the launch traced here: 63.6 us
  blocking collectives  33 us (51%)
  waiting for transfers between devices  17.4 us (27%)
  starting transfers between devices  7.35 us (11%)
  Pallas kernels  3.89 us (6%)
  local copies, waits for them, and re-layouts  1.9 us (3%)
    all_to_all x2, blocking collectives, swap(): lax.all_to_all(value.reshape(owners, -1, *shape[1:]), AXES, split_axis=0,...  33 us
    ppermute x3, waiting for transfers between devices, split_plan(): lax.ppermute(move, AXES, move_pairs(groups, systems, offset))  12.8 us
    ppermute x3, starting transfers between devices, split_plan(): lax.ppermute(move, AXES, move_pairs(groups, systems, offset))  5.41 us
    ppermute x2, waiting for transfers between devices, on_device(): lax.ppermute(own_index, AXES, hub_pairs(groups, systems, offset))  4.61 us
    ppermute x2, starting transfers between devices, on_device(): lax.ppermute(own_index, AXES, hub_pairs(groups, systems, offset))  1.94 us
    unnamed x4, local copies, waits for them, and re-layouts  1.9 us
    pallas_call x1, Pallas kernels, split_plan(): pl.pallas_call(functools.partial(unsort_kernel, systems), out_shape=tiles...  1.6 us
    pallas_call x1, Pallas kernels, split_plan(): pl.pallas_call(functools.partial(sort_kernel, groups, systems, len(hubs))...  1.42 us
  transfers between devices with their start and end apart: 5, of which 3 were waited for; matrix products, arithmetic and copies ran while one was open for 0% of the time, Pallas kernels for 0%

profile of v2, /device:TPU:0, one launch (start us, length us, event | category | flops | bytes accessed | tf_op | source)
XLA Modules:
  0.0 63.6 jit_solution(10460952511286372941)
XLA Ops:
  0.0 0.0 copy-start.1
  0.0 0.7 %copy-done.1 = s32[1,1,32,2]{2,3,1,0:T(2,128)S(1)} copy-done((s32[1,1,32,2]{2,3,1,0:T(2,128)S(1)}, s32[1,1,32,2]{2,3,1,0:T(2,128)}, u32[]{:S(2)}) %copy-start.1) | copy-done | bytes 280
  0.7 1.3 %collective-permute-start.1 = (s32[2,32]{1,0:T(2,128)S(1)}, s32[2,32]{1,0:T(2,128)S(1)}, u32[]{:S(2)}, u32[]{:S(2)}) collective-permute-start(s32[2,32]{1,0:T(2,128)S(1)} %bitcast.15), channel_id=1, source_target_pairs={{3,0},{5,13},{11,9},{6,22},{19,18},{7,31}} | collective-permute-start | bytes 776 | tf_op jit(solution)/shard_map/ppermute | solution.py:392
  2.0 0.7 %collective-permute-start = (s32[2,32]{1,0:T(2,128)S(1)}, s32[2,32]{1,0:T(2,128)S(1)}, u32[]{:S(2)}, u32[]{:S(2)}) collective-permute-start(s32[2,32]{1,0:T(2,128)S(1)} %bitcast.16), channel_id=1, source_target_pairs={{3,1},{5,14},{11,10},{6,23},{19,2},{7,15}} | collective-permute-start | bytes 776 | tf_op jit(solution)/shard_map/ppermute | solution.py:392
  2.6 0.0 copy-start
  2.6 1.2 %copy-done = bf16[1,1,32,128,128]{4,3,2,1,0:T(8,128)(2,1)S(1)} copy-done((bf16[1,1,32,128,128]{4,3,2,1,0:T(8,128)(2,1)S(1)}, bf16[1,1,32,128,128]{4,3,2,1,0:T(8,128)(2,1)}, u32[]{:S(2)}) %copy-start) | copy-done | bytes 1048600
  3.9 0.1 stage_tiles.1.refs_3_
  3.9 4.6 %collective-permute-done.1.refs_2_ = s32[2,32]{1,0:T(2,128)S(1)} collective-permute-done((s32[2,32]{1,0:T(2,128)S(1)}, s32[2,32]{1,0:T(2,128)S(1)}, u32[]{:S(2)}, u32[]{:S(2)}) %collective-permute-start.1) | collective-permute-done | bytes 288 | tf_op jit(solution)/shard_map/ppermute | solution.py:392
  8.5 0.0 collective-permute-done.refs_1_
  8.5 1.4 %sort_by_chain.1 = (bf16[32,128,128]{2,1,0:T(8,128)(2,1)S(1)}, s32[32]{0:T(128)S(1)}) custom-call(s32[2,32]{1,0:T(2,128)S(1)} %bitcast.17, s32[2,32]{1,0:T(2,128)S(1)} %collective-permute-done.refs_1_, s32[2,32]{1,0:T(2,128)S(1)} %collective-permute-done.1.refs_2_, bf16[32,128,128]{2,1,0:T(8,128)(2,1)S(1)} %stage_tiles.1.refs_3_), custom_call_target="tpu_custom_call" | custom-call | tf_op jit(solution)/shard_map/sort_by_chain/pallas_call | solution.py:239
  10.0 12.4 %all_to_all.10 = bf16[4,8,128,128]{3,2,1,0:T(8,128)(2,1)S(1)} all-to-all(bf16[4,8,128,128]{3,2,1,0:T(8,128)(2,1)S(1)} %bitcast.14), channel_id=1, replica_groups={{0,8,16,24},{1,9,17,25},{2,10,18,26},{3,11,19,27},{4,5,6,7},{12,13,14,1..., dimensions={0} | all-to-all | bytes 2097152 | tf_op jit(solution)/shard_map/all_to_all | solution.py:115
  22.3 0.1 pick_moves.1
  22.4 2.2 %collective-permute-start.2 = (bf16[16,128,128]{2,1,0:T(8,128)(2,1)S(1)}, bf16[16,128,128]{2,1,0:T(8,128)(2,1)S(1)}, u32[]{:S(2)}, u32[]{:S(2)}) collective-permute-start(bf16[16,128,128]{2,1,0:T(8,128)(2,1)S(1)} %get-tuple-element.12), channel_id=1, source_target_pairs={{0,1},{1,0},{2,3},{3,2},{8,9},{9,8},{10,11},{11,10},{16,17},{17,16... | collective-permute-start | bytes 1572872 | tf_op jit(solution)/shard_map/ppermute | solution.py:259
  24.6 1.8 %collective-permute-start.3 = (bf16[8,128,128]{2,1,0:T(8,128)(2,1)S(1)}, bf16[8,128,128]{2,1,0:T(8,128)(2,1)S(1)}, u32[]{:S(2)}, u32[]{:S(2)}) collective-permute-start(bf16[8,128,128]{2,1,0:T(8,128)(2,1)S(1)} %get-tuple-element.13), channel_id=1, source_target_pairs={{0,2},{1,3},{2,0},{3,1},{8,10},{9,11},{10,8},{11,9},{16,18},{17,19... | collective-permute-start | bytes 786440 | tf_op jit(solution)/shard_map/ppermute | solution.py:259
  26.4 1.4 %collective-permute-start.4 = (bf16[8,128,128]{2,1,0:T(8,128)(2,1)S(1)}, bf16[8,128,128]{2,1,0:T(8,128)(2,1)S(1)}, u32[]{:S(2)}, u32[]{:S(2)}) collective-permute-start(bf16[8,128,128]{2,1,0:T(8,128)(2,1)S(1)} %get-tuple-element.14), channel_id=1, source_target_pairs={{0,3},{1,2},{2,1},{3,0},{8,11},{9,10},{10,9},{11,8},{16,19},{17,18... | collective-permute-start | bytes 786440 | tf_op jit(solution)/shard_map/ppermute | solution.py:259
  27.8 6.4 %collective-permute-done.3.far_ref = bf16[8,128,128]{2,1,0:T(8,128)(2,1)S(1)} collective-permute-done((bf16[8,128,128]{2,1,0:T(8,128)(2,1)S(1)}, bf16[8,128,128]{2,1,0:T(8,128)(2,1)S(1)}, u32[]{:S(2)}, u32[]{:S(2)}) %collective-permute-start.3) | collective-permute-done | bytes 262176 | tf_op jit(solution)/shard_map/ppermute | solution.py:259
  34.2 6.4 %collective-permute-done.4.far_next_ref = bf16[8,128,128]{2,1,0:T(8,128)(2,1)S(1)} collective-permute-done((bf16[8,128,128]{2,1,0:T(8,128)(2,1)S(1)}, bf16[8,128,128]{2,1,0:T(8,128)(2,1)S(1)}, u32[]{:S(2)}, u32[]{:S(2)}) %collective-permute-start.4) | collective-permute-done | bytes 262176 | tf_op jit(solution)/shard_map/ppermute | solution.py:259
  40.6 0.0 collective-permute-done.2.next_ref
  40.6 0.7 %square_chains.1 = bf16[32,128,128]{2,1,0:T(8,128)(2,1)S(1)} custom-call(bf16[32,128,128]{2,1,0:T(8,128)(2,1)S(1)} %bitcast.10, bf16[16,128,128]{2,1,0:T(8,128)(2,1)S(1)} %collective-permute-done.2.next_ref, bf16[8,128,128]{2,1,0:T(8,128)(2,1)S(1)} %collective-permute-done.3.far_ref, bf16[8,128,128]{2,1,0:T(8,128)(2,1)S(1)} %collective-permute-done.4.far_next_ref), custom_call_target="tpu_custom_call" | custom-call | tf_op jit(solution)/shard_map/square_chains/pallas_call | solution.py:262
  41.3 20.6 %all_to_all.11 = bf16[8,4,128,128]{3,2,1,0:T(8,128)(2,1)S(1)} all-to-all(bf16[8,4,128,128]{3,2,1,0:T(8,128)(2,1)S(1)} %bitcast.11), channel_id=1, replica_groups={{0,1,8,9,16,17,24,25},{4,12,5,13,6,14,7,15},{2,3,10,11,18,19,26,27},{20..., dimensions={0} | all-to-all | bytes 2097152 | tf_op jit(solution)/shard_map/all_to_all | solution.py:115
  61.9 1.6 %back_to_slots.1 = bf16[32,128,128]{2,1,0:T(8,128)(2,1)} custom-call(s32[32]{0:T(128)S(1)} %get-tuple-element.10.slot_ref, bf16[32,128,128]{2,1,0:T(8,128)(2,1)S(1)} %bitcast.12), custom_call_target="tpu_custom_call" | custom-call | tf_op jit(solution)/shard_map/back_to_slots/pallas_call | solution.py:273
Async XLA Ops:
  0.0 0.7 %copy-start.1 = (s32[1,1,32,2]{2,3,1,0:T(2,128)S(1)}, s32[1,1,32,2]{2,3,1,0:T(2,128)}, u32[]{:S(2)}) copy-start(s32[1,1,32,2]{2,3,1,0:T(2,128)} %param.3) | copy-start | bytes 772
  0.7 7.9 %collective-permute-start.1 = (s32[2,32]{1,0:T(2,128)S(1)}, s32[2,32]{1,0:T(2,128)S(1)}, u32[]{:S(2)}, u32[]{:S(2)}) collective-permute-start(s32[2,32]{1,0:T(2,128)S(1)} %bitcast.15), channel_id=1, source_target_pairs={{3,0},{5,13},{11,9},{6,22},{19,18},{7,31}} | collective-permute-start | bytes 776 | tf_op jit(solution)/shard_map/ppermute | solution.py:392
  2.0 6.6 %collective-permute-start = (s32[2,32]{1,0:T(2,128)S(1)}, s32[2,32]{1,0:T(2,128)S(1)}, u32[]{:S(2)}, u32[]{:S(2)}) collective-permute-start(s32[2,32]{1,0:T(2,128)S(1)} %bitcast.16), channel_id=1, source_target_pairs={{3,1},{5,14},{11,10},{6,23},{19,2},{7,15}} | collective-permute-start | bytes 776 | tf_op jit(solution)/shard_map/ppermute | solution.py:392
  2.6 1.2 %copy-start = (bf16[1,1,32,128,128]{4,3,2,1,0:T(8,128)(2,1)S(1)}, bf16[1,1,32,128,128]{4,3,2,1,0:T(8,128)(2,1)}, u32[]{:S(2)}) copy-start(bf16[1,1,32,128,128]{4,3,2,1,0:T(8,128)(2,1)} %param.2) | copy-start | bytes 3145732
  22.4 18.2 %collective-permute-start.2 = (bf16[16,128,128]{2,1,0:T(8,128)(2,1)S(1)}, bf16[16,128,128]{2,1,0:T(8,128)(2,1)S(1)}, u32[]{:S(2)}, u32[]{:S(2)}) collective-permute-start(bf16[16,128,128]{2,1,0:T(8,128)(2,1)S(1)} %get-tuple-element.12), channel_id=1, source_target_pairs={{0,1},{1,0},{2,3},{3,2},{8,9},{9,8},{10,11},{11,10},{16,17},{17,16... | collective-permute-start | bytes 1572872 | tf_op jit(solution)/shard_map/ppermute | solution.py:259
  24.6 9.6 %collective-permute-start.3 = (bf16[8,128,128]{2,1,0:T(8,128)(2,1)S(1)}, bf16[8,128,128]{2,1,0:T(8,128)(2,1)S(1)}, u32[]{:S(2)}, u32[]{:S(2)}) collective-permute-start(bf16[8,128,128]{2,1,0:T(8,128)(2,1)S(1)} %get-tuple-element.13), channel_id=1, source_target_pairs={{0,2},{1,3},{2,0},{3,1},{8,10},{9,11},{10,8},{11,9},{16,18},{17,19... | collective-permute-start | bytes 786440 | tf_op jit(solution)/shard_map/ppermute | solution.py:259
  26.4 14.2 %collective-permute-start.4 = (bf16[8,128,128]{2,1,0:T(8,128)(2,1)S(1)}, bf16[8,128,128]{2,1,0:T(8,128)(2,1)S(1)}, u32[]{:S(2)}, u32[]{:S(2)}) collective-permute-start(bf16[8,128,128]{2,1,0:T(8,128)(2,1)S(1)} %get-tuple-element.14), channel_id=1, source_target_pairs={{0,3},{1,2},{2,1},{3,0},{8,11},{9,10},{10,9},{11,8},{16,19},{17,18... | collective-permute-start | bytes 786440 | tf_op jit(solution)/shard_map/ppermute | solution.py:259

commit v3 on v1

--- a/solution.py
+++ b/solution.py
@@ -20,20 +20,21 @@
     return (v * systems + m) * groups + z
 
 
-def hub_pairs(groups, systems, offset):
-    ring = groups - 1
+def hub_pairs(groups, systems, turn):
+    last = groups - 1
     pairs = []
-    for k in range(ring):
-        partner = (k + offset) % ring
-        if 2 * offset == ring and partner < k:
-            continue
-        low, high = min(k, partner), max(k, partner)
-        for m in range(systems):
-            if kind_of(m) == 0:
-                source, target = (k, ring), (low, high)
-            else:
-                source, target = (0, k + 1), (low + 1, high + 1)
-            pairs.append((device(groups, systems, *source, m), device(groups, systems, *target, m)))
+    for m in range(systems):
+        if kind_of(m) == 0:
+            for v in range(last - turn if turn else last):
+                target = (v, last - turn if turn else v)
+                pairs.append((device(groups, systems, v, last, m), device(groups, systems, *target, m)))
+        elif turn <= last // 2:
+            for k in range(last):
+                partner = (k + turn) % last
+                if 2 * turn == last and partner < k:
+                    continue
+                target = (min(k, partner) + 1, max(k, partner) + 1)
+                pairs.append((device(groups, systems, 0, k + 1, m), device(groups, systems, *target, m)))
     return pairs
 
 
@@ -75,7 +76,8 @@
 def place_of(groups, kind, v, z):
     low = groups // 2
     if kind == 0:
-        return z // low, v * low + z % low
+        half = z // low
+        return half, v * low + (z % low if half else low - 1 - z)
     return v // low, ((1 - z // low) * low + v % low) * low + z % low
 
 
@@ -93,22 +95,12 @@
     return [devices_of(groups, systems, h, m) for h in range(2) for m in range(systems)]
 
 
-def larger_half(m):
-    return 1 - kind_of(m)
-
-
-def cross_pairs(groups, systems, larger):
+def cross_pairs(groups, systems):
     pairs = []
     for m in range(systems):
-        source = larger_half(m) if larger else 1 - larger_half(m)
-        pairs += list(zip(devices_of(groups, systems, source, m), devices_of(groups, systems, 1 - source, m)))
+        halves = [devices_of(groups, systems, h, m) for h in range(2)]
+        pairs += list(zip(*halves)) + list(zip(*halves[::-1]))
     return pairs
-
-
-def sent_places(groups, larger):
-    low = groups // 2
-    stored = [p for p in range(low * low) if p // low <= p % low]
-    return list(range(low * low)) if larger else stored
 
 
 def swap_in_half(value, groups, systems):
@@ -136,7 +128,7 @@
             out_ref[g, q] = tiles_ref[slot_ref[g * share + q]]
 
 
-def split_square_kernel(groups, systems, near_ref, from_larger_ref, from_smaller_ref, out_ref, dense):
+def split_square_kernel(groups, systems, near_ref, far_ref, out_ref, dense):
     low = groups // 2
     spans, share, width = near_ref.shape[:3]
     v, z = lax.axis_index("row") // systems, lax.axis_index("col")
@@ -147,9 +139,6 @@
         return slice(i * width, (i + 1 if j is None else j) * width)
 
     def square(k, h):
-        larger = h == 1 - k
-        far_ref = from_smaller_ref if larger else from_larger_ref
-        arrived = sent_places(groups, not larger)
         for q in range(share):
             for a in range(groups):
                 for b in range(a, groups):
@@ -157,7 +146,7 @@
                     if side == h:
                         tile = near_ref[p, q]
                     elif p < spans // 2:
-                        tile = far_ref[arrived.index(p), q]
+                        tile = far_ref[p, q]
                     else:
                         continue
                     if a == b:
@@ -227,19 +216,16 @@
     )(own_index, *hubs, staged)
 
     near = swap_in_half(by_label, groups, systems)
-    crossing = []
-    for larger in (True, False):
-        sent = jnp.concatenate([near[p : p + 1] for p in sent_places(groups, larger)])
-        crossing.append(lax.ppermute(sent, AXES, cross_pairs(groups, systems, larger)))
+    far = lax.ppermute(near[: spans // 2], AXES, cross_pairs(groups, systems))
     squares = pl.pallas_call(
         functools.partial(split_square_kernel, groups, systems),
         out_shape=by_group,
-        in_specs=[vmem] * 3,
+        in_specs=[vmem] * 2,
         out_specs=vmem,
         scratch_shapes=[pltpu.VMEM((share, groups * width, groups * width), jnp.bfloat16)],
         compiler_params=params,
         name="square_chains",
-    )(near, *crossing)
+    )(near, far)
     returned = swap_in_half(squares, groups, systems)
 
     return pl.pallas_call(
@@ -361,7 +347,7 @@
     slots = own_tiles.shape[0]
     spans = groups * groups // 2
 
-    hubs = [lax.ppermute(own_index, AXES, hub_pairs(groups, systems, offset)) for offset in reversed(range((groups + 1) // 2))]
+    hubs = [lax.ppermute(own_index, AXES, hub_pairs(groups, systems, turn)) for turn in reversed(range(groups - 1))]
     whole_window = groups == STEPS and slots % spans == 0
     plan = split_plan if whole_window else spread_plan
     return plan(own_tiles, own_index, hubs, groups, systems)[None, None]

time: 65.7 us -> 64.6 us (0.983)
  starting transfers between devices: 8.73 us -> 3.62 us
  blocking collectives: 37.2 us -> 40.8 us
    ppermute x4, starting transfers between devices: 8.73 us -> 3.62 us  [the longest x3 2.6 us: on_device(): lax.ppermute(own_index, AXES, hub_pairs(groups, systems, turn))]
    all_to_all x2, blocking collectives: 37.2 us -> 40.8 us  [swap_in_half(): lax.all_to_all(value, AXES, split_axis=0, concat_axis=0, axis_index_group...]
  transfers between devices with their start and end apart: 4 -> 4, of which waited for: 3 -> 2; matrix products, arithmetic and copies ran while one was open for 0% -> 0% of each run, Pallas kernels for 0% -> 0%
where the time goes in v3:
time: 64.6 us; the launch traced here: 64.3 us
  blocking collectives  40.8 us (63%)
  waiting for transfers between devices  14.1 us (22%)
  Pallas kernels  3.8 us (6%)
  starting transfers between devices  3.62 us (6%)
  local copies, waits for them, and re-layouts  1.94 us (3%)
    all_to_all x2, blocking collectives, swap_in_half(): lax.all_to_all(value, AXES, split_axis=0, concat_axis=0, axis_index_group...  40.8 us
    ppermute x1, waiting for transfers between devices, split_plan(): far = lax.ppermute(near[:spans // 2], AXES, cross_pairs(groups, systems))  10.1 us
    ppermute x3, waiting for transfers between devices, on_device(): lax.ppermute(own_index, AXES, hub_pairs(groups, systems, turn))  3.94 us
    ppermute x3, starting transfers between devices, on_device(): lax.ppermute(own_index, AXES, hub_pairs(groups, systems, turn))  2.6 us
    unnamed x4, local copies, waits for them, and re-layouts  1.9 us
    pallas_call x1, Pallas kernels, split_plan(): pl.pallas_call(functools.partial(unsort_kernel, systems), out_shape=regio...  1.6 us
    pallas_call x1, Pallas kernels, split_plan(): pl.pallas_call(functools.partial(sort_kernel, groups, systems, len(hubs))...  1.48 us
  transfers between devices with their start and end apart: 4, of which 2 were waited for; matrix products, arithmetic and copies ran while one was open for 0% of the time, Pallas kernels for 0%

profile of v3, /device:TPU:0, one launch (start us, length us, event | category | flops | bytes accessed | tf_op | source)
XLA Modules:
  0.0 64.3 jit_solution(5487188968255171579)
XLA Ops:
  0.0 0.0 copy-start.1
  0.0 0.7 %copy-done.1 = s32[1,1,32,2]{2,3,1,0:T(2,128)S(1)} copy-done((s32[1,1,32,2]{2,3,1,0:T(2,128)S(1)}, s32[1,1,32,2]{2,3,1,0:T(2,128)}, u32[]{:S(2)}) %copy-start.1) | copy-done | bytes 280
  0.7 1.3 %collective-permute-start.2 = (s32[2,32]{1,0:T(2,128)S(1)}, s32[2,32]{1,0:T(2,128)S(1)}, u32[]{:S(2)}, u32[]{:S(2)}) collective-permute-start(s32[2,32]{1,0:T(2,128)S(1)} %bitcast.6), channel_id=1, source_target_pairs={{3,0},{11,9},{19,18},{5,13},{6,22},{7,31}} | collective-permute-start | bytes 776 | tf_op jit(solution)/shard_map/ppermute | solution.py:350
  2.0 0.7 %collective-permute-start.1 = (s32[2,32]{1,0:T(2,128)S(1)}, s32[2,32]{1,0:T(2,128)S(1)}, u32[]{:S(2)}, u32[]{:S(2)}) collective-permute-start(s32[2,32]{1,0:T(2,128)S(1)} %bitcast.7), channel_id=1, source_target_pairs={{3,2},{11,10},{5,14},{6,23},{7,15}} | collective-permute-start | bytes 776 | tf_op jit(solution)/shard_map/ppermute | solution.py:350
  2.6 0.7 %collective-permute-start = (s32[2,32]{1,0:T(2,128)S(1)}, s32[2,32]{1,0:T(2,128)S(1)}, u32[]{:S(2)}, u32[]{:S(2)}) collective-permute-start(s32[2,32]{1,0:T(2,128)S(1)} %bitcast.8), channel_id=1, source_target_pairs={{3,1}} | collective-permute-start | bytes 776 | tf_op jit(solution)/shard_map/ppermute | solution.py:350
  3.3 0.0 copy-start
  3.3 1.2 %copy-done = bf16[1,1,32,128,128]{4,3,2,1,0:T(8,128)(2,1)S(1)} copy-done((bf16[1,1,32,128,128]{4,3,2,1,0:T(8,128)(2,1)S(1)}, bf16[1,1,32,128,128]{4,3,2,1,0:T(8,128)(2,1)}, u32[]{:S(2)}) %copy-start) | copy-done | bytes 1048600
  4.5 0.1 stage_tiles.1.refs_4_
  4.6 3.9 %collective-permute-done.2.refs_3_ = s32[2,32]{1,0:T(2,128)S(1)} collective-permute-done((s32[2,32]{1,0:T(2,128)S(1)}, s32[2,32]{1,0:T(2,128)S(1)}, u32[]{:S(2)}, u32[]{:S(2)}) %collective-permute-start.2) | collective-permute-done | bytes 288 | tf_op jit(solution)/shard_map/ppermute | solution.py:350
  8.5 0.0 collective-permute-done.1.refs_2_
  8.5 0.0 collective-permute-done.refs_1_
  8.5 1.5 %sort_by_chain.1 = (bf16[8,4,128,128]{3,2,1,0:T(8,128)(2,1)S(1)}, s32[32]{0:T(128)S(1)}) custom-call(s32[2,32]{1,0:T(2,128)S(1)} %bitcast.9, s32[2,32]{1,0:T(2,128)S(1)} %collective-permute-done.refs_1_, s32[2,32]{1,0:T(2,128)S(1)} %collective-permute-done.1.refs_2_, s32[2,32]{1,0:T(2,128)S(1)} %collective-permute-done.2.refs_3_, ...), custom_call_target="tpu_custom_call" | custom-call | tf_op jit(solution)/shard_map/sort_by_chain/pallas_call | solution.py:208
  10.0 20.9 %all_to_all.10.near_ref = bf16[8,4,128,128]{3,2,1,0:T(8,128)(2,1)S(1)} all-to-all(bf16[8,4,128,128]{3,2,1,0:T(8,128)(2,1)S(1)} %get-tuple-element.8), channel_id=1, replica_groups={{1,0,9,8,17,16,25,24},{6,7,14,15,4,5,12,13},{2,3,10,11,18,19,26,27},{22..., dimensions={0} | all-to-all | bytes 2097152 | tf_op jit(solution)/shard_map/all_to_all | solution.py:107
  31.0 1.0 %collective-permute-start.3 = (bf16[4,4,128,128]{3,2,1,0:T(8,128)(2,1)S(1)}, bf16[4,4,128,128]{3,2,1,0:T(8,128)(2,1)S(1)}, u32[]{:S(2)}, u32[]{:S(2)}) collective-permute-start(bf16[4,4,128,128]{3,2,1,0:T(8,128)(2,1)S(1)} %slice.4), channel_id=1, source_target_pairs={{1,2},{0,3},{9,10},{8,11},{17,18},{16,19},{25,26},{24,27},{2,1},{3... | collective-permute-start | bytes 1572872 | tf_op jit(solution)/shard_map/ppermute | solution.py:219
  32.0 10.1 %collective-permute-done.3.far_ref = bf16[4,4,128,128]{3,2,1,0:T(8,128)(2,1)S(1)} collective-permute-done((bf16[4,4,128,128]{3,2,1,0:T(8,128)(2,1)S(1)}, bf16[4,4,128,128]{3,2,1,0:T(8,128)(2,1)S(1)}, u32[]{:S(2)}, u32[]{:S(2)}) %collective-permute-start.3) | collective-permute-done | bytes 524320 | tf_op jit(solution)/shard_map/ppermute | solution.py:219
  42.1 0.6 %square_chains.1 = bf16[8,4,128,128]{3,2,1,0:T(8,128)(2,1)S(1)} custom-call(bf16[8,4,128,128]{3,2,1,0:T(8,128)(2,1)S(1)} %all_to_all.10.near_ref, bf16[4,4,128,128]{3,2,1,0:T(8,128)(2,1)S(1)} %collective-permute-done.3.far_ref), custom_call_target="tpu_custom_call" | custom-call | tf_op jit(solution)/shard_map/square_chains/pallas_call | solution.py:220
  42.8 19.9 %all_to_all.11.sorted_ref = bf16[8,4,128,128]{3,2,1,0:T(8,128)(2,1)S(1)} all-to-all(bf16[8,4,128,128]{3,2,1,0:T(8,128)(2,1)S(1)} %square_chains.1), channel_id=1, replica_groups={{1,0,9,8,17,16,25,24},{6,7,14,15,4,5,12,13},{2,3,10,11,18,19,26,27},{22..., dimensions={0} | all-to-all | bytes 2097152 | tf_op jit(solution)/shard_map/all_to_all | solution.py:107
  62.7 1.6 %back_to_slots.1 = bf16[32,128,128]{2,1,0:T(8,128)(2,1)} custom-call(s32[32]{0:T(128)S(1)} %get-tuple-element.7.slot_ref, bf16[8,4,128,128]{3,2,1,0:T(8,128)(2,1)S(1)} %all_to_all.11.sorted_ref), custom_call_target="tpu_custom_call" | custom-call | tf_op jit(solution)/shard_map/back_to_slots/pallas_call | solution.py:231
  (1 shorter events, 0.0 us)
Async XLA Ops:
  0.0 0.7 %copy-start.1 = (s32[1,1,32,2]{2,3,1,0:T(2,128)S(1)}, s32[1,1,32,2]{2,3,1,0:T(2,128)}, u32[]{:S(2)}) copy-start(s32[1,1,32,2]{2,3,1,0:T(2,128)} %param.3) | copy-start | bytes 772
  0.7 7.9 %collective-permute-start.2 = (s32[2,32]{1,0:T(2,128)S(1)}, s32[2,32]{1,0:T(2,128)S(1)}, u32[]{:S(2)}, u32[]{:S(2)}) collective-permute-start(s32[2,32]{1,0:T(2,128)S(1)} %bitcast.6), channel_id=1, source_target_pairs={{3,0},{11,9},{19,18},{5,13},{6,22},{7,31}} | collective-permute-start | bytes 776 | tf_op jit(solution)/shard_map/ppermute | solution.py:350
  2.0 6.6 %collective-permute-start.1 = (s32[2,32]{1,0:T(2,128)S(1)}, s32[2,32]{1,0:T(2,128)S(1)}, u32[]{:S(2)}, u32[]{:S(2)}) collective-permute-start(s32[2,32]{1,0:T(2,128)S(1)} %bitcast.7), channel_id=1, source_target_pairs={{3,2},{11,10},{5,14},{6,23},{7,15}} | collective-permute-start | bytes 776 | tf_op jit(solution)/shard_map/ppermute | solution.py:350
  2.6 5.9 %collective-permute-start = (s32[2,32]{1,0:T(2,128)S(1)}, s32[2,32]{1,0:T(2,128)S(1)}, u32[]{:S(2)}, u32[]{:S(2)}) collective-permute-start(s32[2,32]{1,0:T(2,128)S(1)} %bitcast.8), channel_id=1, source_target_pairs={{3,1}} | collective-permute-start | bytes 776 | tf_op jit(solution)/shard_map/ppermute | solution.py:350
  3.3 1.2 %copy-start = (bf16[1,1,32,128,128]{4,3,2,1,0:T(8,128)(2,1)S(1)}, bf16[1,1,32,128,128]{4,3,2,1,0:T(8,128)(2,1)}, u32[]{:S(2)}) copy-start(bf16[1,1,32,128,128]{4,3,2,1,0:T(8,128)(2,1)} %param.2) | copy-start | bytes 3145732
  31.0 11.2 %collective-permute-start.3 = (bf16[4,4,128,128]{3,2,1,0:T(8,128)(2,1)S(1)}, bf16[4,4,128,128]{3,2,1,0:T(8,128)(2,1)S(1)}, u32[]{:S(2)}, u32[]{:S(2)}) collective-permute-start(bf16[4,4,128,128]{3,2,1,0:T(8,128)(2,1)S(1)} %slice.4), channel_id=1, source_target_pairs={{1,2},{0,3},{9,10},{8,11},{17,18},{16,19},{25,26},{24,27},{2,1},{3... | collective-permute-start | bytes 1572872 | tf_op jit(solution)/shard_map/ppermute | solution.py:219

commit v4 on v3

--- a/solution.py
+++ b/solution.py
@@ -20,21 +20,20 @@
     return (v * systems + m) * groups + z
 
 
-def hub_pairs(groups, systems, turn):
-    last = groups - 1
+def hub_pairs(groups, systems, offset):
+    ring = groups - 1
     pairs = []
-    for m in range(systems):
-        if kind_of(m) == 0:
-            for v in range(last - turn if turn else last):
-                target = (v, last - turn if turn else v)
-                pairs.append((device(groups, systems, v, last, m), device(groups, systems, *target, m)))
-        elif turn <= last // 2:
-            for k in range(last):
-                partner = (k + turn) % last
-                if 2 * turn == last and partner < k:
-                    continue
-                target = (min(k, partner) + 1, max(k, partner) + 1)
-                pairs.append((device(groups, systems, 0, k + 1, m), device(groups, systems, *target, m)))
+    for k in range(ring):
+        partner = (k + offset) % ring
+        if 2 * offset == ring and partner < k:
+            continue
+        low, high = min(k, partner), max(k, partner)
+        for m in range(systems):
+            if kind_of(m) == 0:
+                source, target = (k, ring), (low, high)
+            else:
+                source, target = (0, k + 1), (low + 1, high + 1)
+            pairs.append((device(groups, systems, *source, m), device(groups, systems, *target, m)))
     return pairs
 
 
@@ -78,7 +77,8 @@
     if kind == 0:
         half = z // low
         return half, v * low + (z % low if half else low - 1 - z)
-    return v // low, ((1 - z // low) * low + v % low) * low + z % low
+    half = v // low
+    return half, ((1 - z // low) * low + (low - 1 - v % low if half else v)) * low + z % low
 
 
 def devices_of(groups, systems, half, m):
@@ -347,7 +347,7 @@
     slots = own_tiles.shape[0]
     spans = groups * groups // 2
 
-    hubs = [lax.ppermute(own_index, AXES, hub_pairs(groups, systems, turn)) for turn in reversed(range(groups - 1))]
+    hubs = [lax.ppermute(own_index, AXES, hub_pairs(groups, systems, offset)) for offset in reversed(range((groups + 1) // 2))]
     whole_window = groups == STEPS and slots % spans == 0
     plan = split_plan if whole_window else spread_plan
     return plan(own_tiles, own_index, hubs, groups, systems)[None, None]

time: 64.6 us -> 63.7 us (0.986)
  blocking collectives: 40.8 us -> 40 us
  starting transfers between devices: 3.62 us -> 2.97 us
    all_to_all x2, blocking collectives: 40.8 us -> 40 us  [swap_in_half(): lax.all_to_all(value, AXES, split_axis=0, concat_axis=0, axis_index_group...]
    ppermute x3 -> x2, waiting for transfers between devices: 3.94 us -> 4.61 us  [on_device(): lax.ppermute(own_index, AXES, hub_pairs(groups, systems, offset))]
    ppermute x3 -> x2, starting transfers between devices: 2.6 us -> 1.94 us  [on_device(): lax.ppermute(own_index, AXES, hub_pairs(groups, systems, offset))]
  transfers between devices with their start and end apart: 4 -> 3, of which waited for: 2 -> 2; matrix products, arithmetic and copies ran while one was open for 0% -> 0% of each run, Pallas kernels for 0% -> 0%
where the time goes in v4:
time: 63.7 us; the launch traced here: 63.4 us
  blocking collectives  40 us (63%)
  waiting for transfers between devices  14.7 us (23%)
  Pallas kernels  3.74 us (6%)
  starting transfers between devices  2.97 us (5%)
  local copies, waits for them, and re-layouts  1.94 us (3%)
    all_to_all x2, blocking collectives, swap_in_half(): lax.all_to_all(value, AXES, split_axis=0, concat_axis=0, axis_index_group...  40 us
    ppermute x1, waiting for transfers between devices, split_plan(): far = lax.ppermute(near[:spans // 2], AXES, cross_pairs(groups, systems))  10.1 us
    ppermute x2, waiting for transfers between devices, on_device(): lax.ppermute(own_index, AXES, hub_pairs(groups, systems, offset))  4.61 us
    ppermute x2, starting transfers between devices, on_device(): lax.ppermute(own_index, AXES, hub_pairs(groups, systems, offset))  1.94 us
    unnamed x4, local copies, waits for them, and re-layouts  1.9 us
    pallas_call x1, Pallas kernels, split_plan(): pl.pallas_call(functools.partial(unsort_kernel, systems), out_shape=regio...  1.6 us
    pallas_call x1, Pallas kernels, split_plan(): pl.pallas_call(functools.partial(sort_kernel, groups, systems, len(hubs))...  1.42 us
  transfers between devices with their start and end apart: 3, of which 2 were waited for; matrix products, arithmetic and copies ran while one was open for 0% of the time, Pallas kernels for 0%

profile of v4, /device:TPU:0, one launch (start us, length us, event | category | flops | bytes accessed | tf_op | source)
XLA Modules:
  0.0 63.4 jit_solution(18287005747232015676)
XLA Ops:
  0.0 0.0 copy-start.1
  0.0 0.7 %copy-done.1 = s32[1,1,32,2]{2,3,1,0:T(2,128)S(1)} copy-done((s32[1,1,32,2]{2,3,1,0:T(2,128)S(1)}, s32[1,1,32,2]{2,3,1,0:T(2,128)}, u32[]{:S(2)}) %copy-start.1) | copy-done | bytes 280
  0.7 1.3 %collective-permute-start.1 = (s32[2,32]{1,0:T(2,128)S(1)}, s32[2,32]{1,0:T(2,128)S(1)}, u32[]{:S(2)}, u32[]{:S(2)}) collective-permute-start(s32[2,32]{1,0:T(2,128)S(1)} %bitcast.6), channel_id=1, source_target_pairs={{3,0},{5,13},{11,9},{6,22},{19,18},{7,31}} | collective-permute-start | bytes 776 | tf_op jit(solution)/shard_map/ppermute | solution.py:350
  2.0 0.7 %collective-permute-start = (s32[2,32]{1,0:T(2,128)S(1)}, s32[2,32]{1,0:T(2,128)S(1)}, u32[]{:S(2)}, u32[]{:S(2)}) collective-permute-start(s32[2,32]{1,0:T(2,128)S(1)} %bitcast.7), channel_id=1, source_target_pairs={{3,1},{5,14},{11,10},{6,23},{19,2},{7,15}} | collective-permute-start | bytes 776 | tf_op jit(solution)/shard_map/ppermute | solution.py:350
  2.6 0.0 copy-start
  2.6 1.2 %copy-done = bf16[1,1,32,128,128]{4,3,2,1,0:T(8,128)(2,1)S(1)} copy-done((bf16[1,1,32,128,128]{4,3,2,1,0:T(8,128)(2,1)S(1)}, bf16[1,1,32,128,128]{4,3,2,1,0:T(8,128)(2,1)}, u32[]{:S(2)}) %copy-start) | copy-done | bytes 1048600
  3.9 0.1 stage_tiles.1.refs_3_
  3.9 4.6 %collective-permute-done.1.refs_2_ = s32[2,32]{1,0:T(2,128)S(1)} collective-permute-done((s32[2,32]{1,0:T(2,128)S(1)}, s32[2,32]{1,0:T(2,128)S(1)}, u32[]{:S(2)}, u32[]{:S(2)}) %collective-permute-start.1) | collective-permute-done | bytes 288 | tf_op jit(solution)/shard_map/ppermute | solution.py:350
  8.5 0.0 collective-permute-done.refs_1_
  8.5 1.4 %sort_by_chain.1 = (bf16[8,4,128,128]{3,2,1,0:T(8,128)(2,1)S(1)}, s32[32]{0:T(128)S(1)}) custom-call(s32[2,32]{1,0:T(2,128)S(1)} %bitcast.8, s32[2,32]{1,0:T(2,128)S(1)} %collective-permute-done.refs_1_, s32[2,32]{1,0:T(2,128)S(1)} %collective-permute-done.1.refs_2_, bf16[32,128,128]{2,1,0:T(8,128)(2,1)S(1)} %stage_tiles.1.refs_3_), custom_call_target="tpu_custom_call" | custom-call | tf_op jit(solution)/shard_map/sort_by_chain/pallas_call | solution.py:208
  10.0 20.9 %all_to_all.10.near_ref = bf16[8,4,128,128]{3,2,1,0:T(8,128)(2,1)S(1)} all-to-all(bf16[8,4,128,128]{3,2,1,0:T(8,128)(2,1)S(1)} %get-tuple-element.8), channel_id=1, replica_groups={{1,0,9,8,17,16,25,24},{6,7,14,15,4,5,12,13},{2,3,10,11,18,19,26,27},{30..., dimensions={0} | all-to-all | bytes 2097152 | tf_op jit(solution)/shard_map/all_to_all | solution.py:107
  30.9 1.0 %collective-permute-start.2 = (bf16[4,4,128,128]{3,2,1,0:T(8,128)(2,1)S(1)}, bf16[4,4,128,128]{3,2,1,0:T(8,128)(2,1)S(1)}, u32[]{:S(2)}, u32[]{:S(2)}) collective-permute-start(bf16[4,4,128,128]{3,2,1,0:T(8,128)(2,1)S(1)} %slice.4), channel_id=1, source_target_pairs={{1,2},{0,3},{9,10},{8,11},{17,18},{16,19},{25,26},{24,27},{2,1},{3... | collective-permute-start | bytes 1572872 | tf_op jit(solution)/shard_map/ppermute | solution.py:219
  32.0 10.1 %collective-permute-done.2.far_ref = bf16[4,4,128,128]{3,2,1,0:T(8,128)(2,1)S(1)} collective-permute-done((bf16[4,4,128,128]{3,2,1,0:T(8,128)(2,1)S(1)}, bf16[4,4,128,128]{3,2,1,0:T(8,128)(2,1)S(1)}, u32[]{:S(2)}, u32[]{:S(2)}) %collective-permute-start.2) | collective-permute-done | bytes 524320 | tf_op jit(solution)/shard_map/ppermute | solution.py:219
  42.1 0.7 %square_chains.1 = bf16[8,4,128,128]{3,2,1,0:T(8,128)(2,1)S(1)} custom-call(bf16[8,4,128,128]{3,2,1,0:T(8,128)(2,1)S(1)} %all_to_all.10.near_ref, bf16[4,4,128,128]{3,2,1,0:T(8,128)(2,1)S(1)} %collective-permute-done.2.far_ref), custom_call_target="tpu_custom_call" | custom-call | tf_op jit(solution)/shard_map/square_chains/pallas_call | solution.py:220
  42.8 19.0 %all_to_all.11.sorted_ref = bf16[8,4,128,128]{3,2,1,0:T(8,128)(2,1)S(1)} all-to-all(bf16[8,4,128,128]{3,2,1,0:T(8,128)(2,1)S(1)} %square_chains.1), channel_id=1, replica_groups={{1,0,9,8,17,16,25,24},{6,7,14,15,4,5,12,13},{2,3,10,11,18,19,26,27},{30..., dimensions={0} | all-to-all | bytes 2097152 | tf_op jit(solution)/shard_map/all_to_all | solution.py:107
  61.8 1.6 %back_to_slots.1 = bf16[32,128,128]{2,1,0:T(8,128)(2,1)} custom-call(s32[32]{0:T(128)S(1)} %get-tuple-element.7.slot_ref, bf16[8,4,128,128]{3,2,1,0:T(8,128)(2,1)S(1)} %all_to_all.11.sorted_ref), custom_call_target="tpu_custom_call" | custom-call | tf_op jit(solution)/shard_map/back_to_slots/pallas_call | solution.py:231
  (1 shorter events, 0.0 us)
Async XLA Ops:
  0.0 0.7 %copy-start.1 = (s32[1,1,32,2]{2,3,1,0:T(2,128)S(1)}, s32[1,1,32,2]{2,3,1,0:T(2,128)}, u32[]{:S(2)}) copy-start(s32[1,1,32,2]{2,3,1,0:T(2,128)} %param.3) | copy-start | bytes 772
  0.7 7.9 %collective-permute-start.1 = (s32[2,32]{1,0:T(2,128)S(1)}, s32[2,32]{1,0:T(2,128)S(1)}, u32[]{:S(2)}, u32[]{:S(2)}) collective-permute-start(s32[2,32]{1,0:T(2,128)S(1)} %bitcast.6), channel_id=1, source_target_pairs={{3,0},{5,13},{11,9},{6,22},{19,18},{7,31}} | collective-permute-start | bytes 776 | tf_op jit(solution)/shard_map/ppermute | solution.py:350
  2.0 6.6 %collective-permute-start = (s32[2,32]{1,0:T(2,128)S(1)}, s32[2,32]{1,0:T(2,128)S(1)}, u32[]{:S(2)}, u32[]{:S(2)}) collective-permute-start(s32[2,32]{1,0:T(2,128)S(1)} %bitcast.7), channel_id=1, source_target_pairs={{3,1},{5,14},{11,10},{6,23},{19,2},{7,15}} | collective-permute-start | bytes 776 | tf_op jit(solution)/shard_map/ppermute | solution.py:350
  2.6 1.2 %copy-start = (bf16[1,1,32,128,128]{4,3,2,1,0:T(8,128)(2,1)S(1)}, bf16[1,1,32,128,128]{4,3,2,1,0:T(8,128)(2,1)}, u32[]{:S(2)}) copy-start(bf16[1,1,32,128,128]{4,3,2,1,0:T(8,128)(2,1)} %param.2) | copy-start | bytes 3145732
  30.9 11.2 %collective-permute-start.2 = (bf16[4,4,128,128]{3,2,1,0:T(8,128)(2,1)S(1)}, bf16[4,4,128,128]{3,2,1,0:T(8,128)(2,1)S(1)}, u32[]{:S(2)}, u32[]{:S(2)}) collective-permute-start(bf16[4,4,128,128]{3,2,1,0:T(8,128)(2,1)S(1)} %slice.4), channel_id=1, source_target_pairs={{1,2},{0,3},{9,10},{8,11},{17,18},{16,19},{25,26},{24,27},{2,1},{3... | collective-permute-start | bytes 1572872 | tf_op jit(solution)/shard_map/ppermute | solution.py:219

commit v5 on v4

--- a/solution.py
+++ b/solution.py
@@ -77,8 +77,7 @@
     if kind == 0:
         half = z // low
         return half, v * low + (z % low if half else low - 1 - z)
-    half = v // low
-    return half, ((1 - z // low) * low + (low - 1 - v % low if half else v)) * low + z % low
+    return v // low, ((1 - z // low) * low + v % low) * low + z % low
 
 
 def devices_of(groups, systems, half, m):
@@ -128,46 +127,63 @@
             out_ref[g, q] = tiles_ref[slot_ref[g * share + q]]
 
 
-def split_square_kernel(groups, systems, near_ref, far_ref, out_ref, dense):
+def each_half(groups, systems, body):
     low = groups // 2
-    spans, share, width = near_ref.shape[:3]
     v, z = lax.axis_index("row") // systems, lax.axis_index("col")
     kind = kind_of(lax.axis_index("row") % systems)
     half = jnp.where(kind == 0, z, v) // low
+    for k in sorted({kind_of(m) for m in range(systems)}):
+        for h in range(2):
+            pl.when((kind == k) & (half == h))(functools.partial(body, k, h))
+
+
+def fill(groups, k, h, own, tiles_ref, dense_ref):
+    spans, share, width = groups * groups // 2, tiles_ref.shape[1], tiles_ref.shape[2]
+
+    def at(i):
+        return slice(i * width, (i + 1) * width)
+
+    for q in range(share):
+        for a in range(groups):
+            for b in range(a, groups):
+                side, p = place_of(groups, k, a, b)
+                if (side == h) != own or (not own and p >= spans // 2):
+                    continue
+                tile = tiles_ref[p, q]
+                if a == b:
+                    dense_ref[q, at(a), at(a)] = symmetric(tile)
+                else:
+                    dense_ref[q, at(a), at(b)] = tile
+                    dense_ref[q, at(b), at(a)] = tile.T
+
+
+def fill_kernel(groups, systems, near_ref, dense_ref):
+    each_half(groups, systems, lambda k, h: fill(groups, k, h, True, near_ref, dense_ref))
+
+
+def split_square_kernel(groups, systems, near_dense_ref, far_ref, out_ref, dense_ref):
+    low = groups // 2
+    share, width = far_ref.shape[1], far_ref.shape[2]
 
     def at(i, j=None):
         return slice(i * width, (i + 1 if j is None else j) * width)
 
     def square(k, h):
+        dense_ref[...] = near_dense_ref[...]
+        fill(groups, k, h, False, far_ref, dense_ref)
+        if k == 0:
+            rows, columns = (0, (h + 1) * low), (h * low, (h + 1) * low)
+        else:
+            rows, columns = (h * low, (h + 1) * low), (h * low, groups)
         for q in range(share):
-            for a in range(groups):
-                for b in range(a, groups):
-                    side, p = place_of(groups, k, a, b)
-                    if side == h:
-                        tile = near_ref[p, q]
-                    elif p < spans // 2:
-                        tile = far_ref[p, q]
-                    else:
-                        continue
-                    if a == b:
-                        dense[q, at(a), at(a)] = symmetric(tile)
-                    else:
-                        dense[q, at(a), at(b)] = tile
-                        dense[q, at(b), at(a)] = tile.T
-            if k == 0:
-                rows, columns = (0, (h + 1) * low), (h * low, (h + 1) * low)
-            else:
-                rows, columns = (h * low, (h + 1) * low), (h * low, groups)
             product = jnp.dot(
-                dense[q, at(*rows), :], dense[q, :, at(*columns)], preferred_element_type=jnp.float32
+                dense_ref[q, at(*rows), :], dense_ref[q, :, at(*columns)], preferred_element_type=jnp.float32
             ).astype(jnp.bfloat16)
             for a in range(*rows):
                 for b in range(max(a, columns[0]), columns[1]):
                     out_ref[place_of(groups, k, a, b)[1], q] = product[at(a - rows[0]), at(b - columns[0])]
 
-    for k in range(min(systems, 2)):
-        for h in range(2):
-            pl.when((kind == k) & (half == h))(functools.partial(square, k, h))
+    each_half(groups, systems, square)
 
 
 def unsort_kernel(systems, slot_ref, sorted_ref, out_ref):
@@ -217,15 +233,26 @@
 
     near = swap_in_half(by_label, groups, systems)
     far = lax.ppermute(near[: spans // 2], AXES, cross_pairs(groups, systems))
+    side = groups * width
+    dense = jax.ShapeDtypeStruct((share, side, side), jnp.bfloat16)
+    own_dense = pl.pallas_call(
+        functools.partial(fill_kernel, groups, systems),
+        out_shape=dense,
+        in_specs=[vmem],
+        out_specs=vmem,
+        compiler_params=params,
+        cost_estimate=pl.CostEstimate(flops=0, bytes_accessed=2 * share * side * side, transcendentals=0),
+        name="lay_out_own",
+    )(near)
     squares = pl.pallas_call(
         functools.partial(split_square_kernel, groups, systems),
         out_shape=by_group,
         in_specs=[vmem] * 2,
         out_specs=vmem,
-        scratch_shapes=[pltpu.VMEM((share, groups * width, groups * width), jnp.bfloat16)],
+        scratch_shapes=[pltpu.VMEM(dense.shape, jnp.bfloat16)],
         compiler_params=params,
         name="square_chains",
-    )(near, far)
+    )(own_dense, far)
     returned = swap_in_half(squares, groups, systems)
 
     return pl.pallas_call(

time: 63.7 us -> 62.6 us (0.983)
  blocking collectives: 40 us -> 39.3 us
  local copies, waits for them, and re-layouts: 1.94 us -> 1.26 us
    all_to_all x2, blocking collectives: 40 us -> 39.3 us  [swap_in_half(): lax.all_to_all(value, AXES, split_axis=0, concat_axis=0, axis_index_group...]
    unnamed x4, local copies, waits for them, and re-layouts: 1.9 us -> 1.22 us
where the time goes in v5:
time: 62.6 us; the launch traced here: 62.3 us
  blocking collectives  39.3 us (63%)
  waiting for transfers between devices  14.7 us (23%)
  Pallas kernels  3.9 us (6%)
  starting transfers between devices  3.16 us (5%)
  local copies, waits for them, and re-layouts  1.26 us (2%)
    all_to_all x2, blocking collectives, swap_in_half(): lax.all_to_all(value, AXES, split_axis=0, concat_axis=0, axis_index_group...  39.3 us
    ppermute x1, waiting for transfers between devices, split_plan(): far = lax.ppermute(near[:spans // 2], AXES, cross_pairs(groups, systems))  9.86 us
    ppermute x2, waiting for transfers between devices, on_device(): lax.ppermute(own_index, AXES, hub_pairs(groups, systems, offset))  4.82 us
    ppermute x2, starting transfers between devices, on_device(): lax.ppermute(own_index, AXES, hub_pairs(groups, systems, offset))  2.07 us
    pallas_call x1, Pallas kernels, split_plan(): pl.pallas_call(functools.partial(unsort_kernel, systems), out_shape=regio...  1.6 us
    pallas_call x1, Pallas kernels, split_plan(): pl.pallas_call(functools.partial(sort_kernel, groups, systems, len(hubs))...  1.42 us
  transfers between devices with their start and end apart: 3, of which 2 were waited for; matrix products, arithmetic and copies ran while one was open for 0% of the time, Pallas kernels for 0%

profile of v5, /device:TPU:0, one launch (start us, length us, event | category | flops | bytes accessed | tf_op | source)
XLA Modules:
  0.0 62.3 jit_solution(660582813572304097)
XLA Ops:
  0.0 0.0 copy-start.1
  0.0 1.4 %collective-permute-start.1 = (s32[2,32]{1,0:T(2,128)}, s32[2,32]{1,0:T(2,128)S(1)}, u32[]{:S(2)}, u32[]{:S(2)}) collective-permute-start(s32[2,32]{1,0:T(2,128)} %bitcast.6), channel_id=1, source_target_pairs={{3,0},{5,13},{11,9},{6,22},{19,18},{7,31}} | collective-permute-start | bytes 776 | tf_op jit(solution)/shard_map/ppermute | solution.py:377
  1.4 0.7 %collective-permute-start = (s32[2,32]{1,0:T(2,128)}, s32[2,32]{1,0:T(2,128)S(1)}, u32[]{:S(2)}, u32[]{:S(2)}) collective-permute-start(s32[2,32]{1,0:T(2,128)} %bitcast.7), channel_id=1, source_target_pairs={{3,1},{5,14},{11,10},{6,23},{19,2},{7,15}} | collective-permute-start | bytes 776 | tf_op jit(solution)/shard_map/ppermute | solution.py:377
  2.1 0.0 copy-start
  2.1 1.2 %copy-done = bf16[1,1,32,128,128]{4,3,2,1,0:T(8,128)(2,1)S(1)} copy-done((bf16[1,1,32,128,128]{4,3,2,1,0:T(8,128)(2,1)S(1)}, bf16[1,1,32,128,128]{4,3,2,1,0:T(8,128)(2,1)}, u32[]{:S(2)}) %copy-start) | copy-done | bytes 1048600
  3.3 0.1 stage_tiles.1.refs_3_
  3.4 4.8 %collective-permute-done.1.refs_2_ = s32[2,32]{1,0:T(2,128)S(1)} collective-permute-done((s32[2,32]{1,0:T(2,128)}, s32[2,32]{1,0:T(2,128)S(1)}, u32[]{:S(2)}, u32[]{:S(2)}) %collective-permute-start.1) | collective-permute-done | bytes 288 | tf_op jit(solution)/shard_map/ppermute | solution.py:377
  8.2 0.0 collective-permute-done.refs_1_
  8.2 0.0 copy-done.1
  8.2 1.4 %sort_by_chain.1 = (bf16[8,4,128,128]{3,2,1,0:T(8,128)(2,1)S(1)}, s32[32]{0:T(128)S(1)}) custom-call(s32[2,32]{1,0:T(2,128)S(1)} %bitcast.8, s32[2,32]{1,0:T(2,128)S(1)} %collective-permute-done.refs_1_, s32[2,32]{1,0:T(2,128)S(1)} %collective-permute-done.1.refs_2_, bf16[32,128,128]{2,1,0:T(8,128)(2,1)S(1)} %stage_tiles.1.refs_3_), custom_call_target="tpu_custom_call" | custom-call | tf_op jit(solution)/shard_map/sort_by_chain/pallas_call | solution.py:224
  9.6 20.8 %all_to_all.10.near_ref = bf16[8,4,128,128]{3,2,1,0:T(8,128)(2,1)S(1)} all-to-all(bf16[8,4,128,128]{3,2,1,0:T(8,128)(2,1)S(1)} %get-tuple-element.8), channel_id=1, replica_groups={{1,0,9,8,17,16,25,24},{6,7,14,15,4,5,12,13},{2,3,10,11,18,19,26,27},{22..., dimensions={0} | all-to-all | bytes 2097152 | tf_op jit(solution)/shard_map/all_to_all | solution.py:106
  30.5 1.1 %collective-permute-start.2 = (bf16[4,4,128,128]{3,2,1,0:T(8,128)(2,1)S(1)}, bf16[4,4,128,128]{3,2,1,0:T(8,128)(2,1)S(1)}, u32[]{:S(2)}, u32[]{:S(2)}) collective-permute-start(bf16[4,4,128,128]{3,2,1,0:T(8,128)(2,1)S(1)} %slice.4), channel_id=1, source_target_pairs={{1,2},{0,3},{9,10},{8,11},{17,18},{16,19},{25,26},{24,27},{2,1},{3... | collective-permute-start | bytes 1572872 | tf_op jit(solution)/shard_map/ppermute | solution.py:235
  31.6 0.2 lay_out_own.1.near_dense_ref
  31.8 9.9 %collective-permute-done.2.far_ref = bf16[4,4,128,128]{3,2,1,0:T(8,128)(2,1)S(1)} collective-permute-done((bf16[4,4,128,128]{3,2,1,0:T(8,128)(2,1)S(1)}, bf16[4,4,128,128]{3,2,1,0:T(8,128)(2,1)S(1)}, u32[]{:S(2)}, u32[]{:S(2)}) %collective-permute-start.2) | collective-permute-done | bytes 524320 | tf_op jit(solution)/shard_map/ppermute | solution.py:235
  41.6 0.6 square_chains.1
  42.2 18.5 %all_to_all.11.sorted_ref = bf16[8,4,128,128]{3,2,1,0:T(8,128)(2,1)S(1)} all-to-all(bf16[8,4,128,128]{3,2,1,0:T(8,128)(2,1)S(1)} %square_chains.1), channel_id=1, replica_groups={{1,0,9,8,17,16,25,24},{6,7,14,15,4,5,12,13},{2,3,10,11,18,19,26,27},{22..., dimensions={0} | all-to-all | bytes 2097152 | tf_op jit(solution)/shard_map/all_to_all | solution.py:106
  60.7 1.6 %back_to_slots.1 = bf16[32,128,128]{2,1,0:T(8,128)(2,1)} custom-call(s32[32]{0:T(128)S(1)} %get-tuple-element.7.slot_ref, bf16[8,4,128,128]{3,2,1,0:T(8,128)(2,1)S(1)} %all_to_all.11.sorted_ref), custom_call_target="tpu_custom_call" | custom-call | tf_op jit(solution)/shard_map/back_to_slots/pallas_call | solution.py:258
  (1 shorter events, 0.0 us)
Async XLA Ops:
  0.0 8.2 %copy-start.1 = (s32[1,1,32,2]{2,3,1,0:T(2,128)S(1)}, s32[1,1,32,2]{2,3,1,0:T(2,128)}, u32[]{:S(2)}) copy-start(s32[1,1,32,2]{2,3,1,0:T(2,128)} %param.3) | copy-start | bytes 772
  0.0 8.2 %collective-permute-start.1 = (s32[2,32]{1,0:T(2,128)}, s32[2,32]{1,0:T(2,128)S(1)}, u32[]{:S(2)}, u32[]{:S(2)}) collective-permute-start(s32[2,32]{1,0:T(2,128)} %bitcast.6), channel_id=1, source_target_pairs={{3,0},{5,13},{11,9},{6,22},{19,18},{7,31}} | collective-permute-start | bytes 776 | tf_op jit(solution)/shard_map/ppermute | solution.py:377
  1.4 6.8 %collective-permute-start = (s32[2,32]{1,0:T(2,128)}, s32[2,32]{1,0:T(2,128)S(1)}, u32[]{:S(2)}, u32[]{:S(2)}) collective-permute-start(s32[2,32]{1,0:T(2,128)} %bitcast.7), channel_id=1, source_target_pairs={{3,1},{5,14},{11,10},{6,23},{19,2},{7,15}} | collective-permute-start | bytes 776 | tf_op jit(solution)/shard_map/ppermute | solution.py:377
  2.1 1.2 %copy-start = (bf16[1,1,32,128,128]{4,3,2,1,0:T(8,128)(2,1)S(1)}, bf16[1,1,32,128,128]{4,3,2,1,0:T(8,128)(2,1)}, u32[]{:S(2)}) copy-start(bf16[1,1,32,128,128]{4,3,2,1,0:T(8,128)(2,1)} %param.2) | copy-start | bytes 3145732
  30.5 11.1 %collective-permute-start.2 = (bf16[4,4,128,128]{3,2,1,0:T(8,128)(2,1)S(1)}, bf16[4,4,128,128]{3,2,1,0:T(8,128)(2,1)S(1)}, u32[]{:S(2)}, u32[]{:S(2)}) collective-permute-start(bf16[4,4,128,128]{3,2,1,0:T(8,128)(2,1)S(1)} %slice.4), channel_id=1, source_target_pairs={{1,2},{0,3},{9,10},{8,11},{17,18},{16,19},{25,26},{24,27},{2,1},{3... | collective-permute-start | bytes 1572872 | tf_op jit(solution)/shard_map/ppermute | solution.py:235
